TPU v7x, 512 devices: a whole 4x4x16 slice. The times are simulated.
512 devices in a mesh: gx: 16 (over z_lo, core), gy: 32 (over z_hi, y, x).
Axes of the slice: x: 4, y: 4, z: 16 (z_hi: 2, z_lo: 8; z = z_hi * 8 + z_lo), core: 2. Of those that a mesh axis runs over, the one named last changes fastest.
Arguments:
- c_upper: bfloat16 [16, 32, 96, 96], P('gx', 'gy'), may hold values from -60 to 60
- edge_upper: bfloat16 [16, 32, 96, 1536], P('gx', 'gy'), may hold values from -60 to 60
- edge_left: bfloat16 [16, 32, 96, 1536], P('gx', 'gy'), may hold values from -60 to 60
- c_lower: bfloat16 [16, 32, 96, 96], P('gx', 'gy'), may hold values from -60 to 60
- edge_lower: bfloat16 [16, 32, 96, 1536], P('gx', 'gy'), may hold values from -60 to 60
- site_ket: bfloat16 [16, 32, 2, 256], P('gx', 'gy'), may hold values from -6 to 6
- time_gate: float32 [2, 2], replicated, may hold values from -3 to 3
- quench_sites: int32 [4], replicated, may hold values from 0 to 511
Outputs:
- new_c_upper: bfloat16 [16, 32, 96, 96], P('gx', 'gy')
- new_edge_left: bfloat16 [16, 32, 96, 1536], P('gx', 'gy')
- new_c_lower: bfloat16 [16, 32, 96, 96], P('gx', 'gy')
All inputs are finite; a program needn't handle non-finite values.
Results may differ from a plain program's by a relative error of at most 0.03.
Values may be sent and summed in bfloat16 or wider, within the bound.
A program may use at most 64 MiB of HBM per device.

v0:
```python
import math

import jax
import jax.numpy as jnp
from jax import lax
from jax.sharding import PartitionSpec as P

NS_ITERS = 6
STEPS = 2


def passed_along(shard, axis, by):
    peers = lax.axis_size(axis)
    return lax.ppermute(shard, axis, [(i, (i + by) % peers) for i in range(peers)])


def polar_factor(matrix):
    scale = jnp.sqrt(jnp.sum(matrix * matrix) + 1e-06)
    iterate = matrix / scale
    for sweep in range(NS_ITERS):
        gram = jnp.dot(iterate.T, iterate, precision=lax.Precision.HIGHEST)
        iterate = 1.5 * iterate - 0.5 * jnp.dot(iterate, gram, precision=lax.Precision.HIGHEST)
    return iterate


def unit_scaled(tensor):
    return tensor / jnp.sqrt(jnp.mean(tensor * tensor) + 1e-06)


def per_device(
    c_upper, edge_upper, edge_left, c_lower, edge_lower, site_ket, time_gate, quench_sites
):
    env_width = c_upper.shape[-1]
    double_bond = edge_upper.shape[-1] // env_width
    bond_dim = math.isqrt(double_bond)
    phys_dim = site_ket.shape[2]
    ket_sites = site_ket[0, 0].reshape(phys_dim, bond_dim, bond_dim, bond_dim, bond_dim)
    gram = jnp.dot(time_gate.T, time_gate, precision=lax.Precision.HIGHEST)
    gated = jnp.einsum(
        "st,tabcd->sabcd", gram, ket_sites.astype(jnp.float32), precision=lax.Precision.HIGHEST
    )
    own_index = lax.axis_index("gx") * lax.axis_size("gy") + lax.axis_index("gy")
    chosen = jnp.any(quench_sites == own_index)
    bra = jnp.where(chosen, gated, ket_sites.astype(jnp.float32)).astype(jnp.bfloat16)
    north_edge = edge_upper[0, 0]
    south_edge = edge_lower[0, 0]
    corner_up = c_upper[0, 0]
    west_edge = edge_left[0, 0]
    corner_low = c_lower[0, 0]
    block = math.gcd(env_width, 16)
    starts = jnp.arange(env_width // block, dtype=jnp.int32) * block
    for step in range(STEPS):
        upper = jnp.dot(corner_up, north_edge, preferred_element_type=jnp.float32).reshape(
            env_width * double_bond, env_width
        )
        lower = jnp.dot(corner_low, south_edge, preferred_element_type=jnp.float32).reshape(
            env_width * double_bond, env_width
        )
        from_below = passed_along(upper.astype(jnp.bfloat16), "gy", -1).astype(upper.dtype)
        proj_below = polar_factor(lower + from_below)
        proj_above = passed_along(proj_below.astype(jnp.bfloat16), "gy", 1).astype(proj_below.dtype)
        low_half = proj_below.astype(jnp.bfloat16).reshape(env_width, double_bond, env_width)
        up_half = proj_above.astype(jnp.bfloat16).reshape(env_width, bond_dim, bond_dim, env_width)
        west = west_edge.reshape(env_width, double_bond, env_width)

        def one_block(start):
            columns = lax.dynamic_slice_in_dim(low_half, start, block, 2)
            first = jnp.einsum(
                "ulw,wdj->uldj", west, columns, preferred_element_type=jnp.float32
            ).astype(jnp.bfloat16)
            first = first.reshape(env_width, bond_dim, bond_dim, bond_dim, bond_dim, block)
            second = jnp.einsum(
                "uaebfj,sagcb->uefjsgc", first, ket_sites, preferred_element_type=jnp.float32
            ).astype(jnp.bfloat16)
            third = jnp.einsum(
                "uefjsgc,sehkf->ughckj", second, bra, preferred_element_type=jnp.float32
            ).astype(jnp.bfloat16)
            return jnp.einsum(
                "ughi,ughckj->jick", up_half, third, preferred_element_type=jnp.float32
            )

        pieces = lax.map(one_block, starts)
        edge_new = pieces.reshape(env_width, env_width, bond_dim, bond_dim)
        edge_new = jnp.transpose(edge_new, (1, 2, 3, 0)).reshape(env_width, double_bond * env_width)
        edge_new = unit_scaled(edge_new).astype(jnp.bfloat16)
        new_up = jnp.dot(proj_above.T, upper, precision=lax.Precision.HIGHEST)
        new_low = jnp.dot(proj_below.T, lower, precision=lax.Precision.HIGHEST)
        new_up = unit_scaled(new_up).astype(jnp.bfloat16)
        new_low = unit_scaled(new_low).astype(jnp.bfloat16)
        corner_up, west_edge, corner_low = passed_along((new_up, edge_new, new_low), "gx", 1)
    return (corner_up[None, None], west_edge[None, None], corner_low[None, None])


def solution(mesh):
    return jax.shard_map(
        per_device,
        mesh=mesh,
        in_specs=(
            P("gx", "gy", None, None),
            P("gx", "gy", None, None),
            P("gx", "gy", None, None),
            P("gx", "gy", None, None),
            P("gx", "gy", None, None),
            P("gx", "gy", None, None),
            P(),
            P(),
        ),
        out_specs=(P("gx", "gy", None, None), P("gx", "gy", None, None), P("gx", "gy", None, None)),
        check_vma=False,
    )
```

profile of v0, /device:TPU:1, one launch (start us, length us, event | category | flops | bytes accessed | tf_op | source)
XLA Modules:
  0.0 281.2 jit_solution(9661263330166529302)
XLA Ops:
  3.0 20.9 %collective-permute-start = (bf16[1536,96]{0,1:T(8,128)(2,1)S(1)}, bf16[1536,96]{0,1:T(8,128)(2,1)S(1)}, u32[]{:S(2)}, u32[]{:S(2)}) collective-permute-start(bf16[1536,96]{0,1:T(8,128)(2,1)S(1)} %copy.49), channel_id=1, source_target_pairs={{0,31},{1,0},{2,1},{3,2},{4,3},{5,4},{6,5},{7,6},{8,7},{9,8},{10,9... | collective-permute-start | bytes 884744 | tf_op jit(solution)/shard_map/ppermute | solution.py:14
  26.6 21.7 %collective-permute-done = bf16[1536,96]{0,1:T(8,128)(2,1)S(1)} collective-permute-done((bf16[1536,96]{0,1:T(8,128)(2,1)S(1)}, bf16[1536,96]{0,1:T(8,128)(2,1)S(1)}, u32[]{:S(2)}, u32[]{:S(2)}) %collective-permute-start) | collective-permute-done | bytes 294944 | tf_op jit(solution)/shard_map/ppermute | solution.py:14
  58.7 1.9 collective-permute-start.2
  63.5 1.9 multiply_reduce_fusion.7
  66.6 24.3 %collective-permute-done.2 = bf16[1536,96]{0,1:T(8,128)(2,1)} collective-permute-done((bf16[1536,96]{0,1:T(8,128)(2,1)}, bf16[1536,96]{0,1:T(8,128)(2,1)}, u32[]{:S(2)}, u32[]{:S(2)}) %collective-permute-start.2) | collective-permute-done | bytes 294944 | tf_op jit(solution)/shard_map/ppermute | solution.py:14
  90.8 2.0 multiply_reduce_fusion.6
  93.6 3.8 %collective-permute-start.3 = (bf16[96,96]{1,0:T(8,128)(2,1)S(1)}, bf16[96,96]{1,0:T(8,128)(2,1)S(1)}, u32[]{:S(2)}, u32[]{:S(2)}) collective-permute-start(bf16[96,96]{1,0:T(8,128)(2,1)S(1)} %divide_convert_fusion.2), channel_id=1, source_target_pairs={{0,32},{32,64},{64,96},{96,128},{128,160},{160,192},{192,224},{224... | collective-permute-start | bytes 55304 | tf_op jit(solution)/shard_map/ppermute | solution.py:14
  98.8 46.4 %while.20 = (s32[]{:T(128)}, f32[6,16,96,4,4]{2,1,4,3,0:T(8,128)S(1)}, s32[6]{0:T(128)S(1)}, bf16[96,16,96]{0,2,1:T(8,128)(2,1)S(1)}, bf16[96,16,96]{2,0,1:T(8,1...) while((s32[]{:T(128)}, ...), condition=%wide.region_7.8_spmd, body=%wide.region_6.7_spmd.sunk | while | flops 202899456 | bytes 7538859 | solution.py:82
  103.6 2.0 fusion.166
  111.3 2.0 fusion.166
  119.1 2.0 fusion.166
  126.8 2.0 fusion.166
  134.6 2.0 fusion.166
  142.3 2.0 fusion.166
  147.0 1.9 collective-permute-start.7
  150.3 1.9 collective-permute-start.4
  152.2 1.9 collective-permute-start.1
  154.2 14.6 %collective-permute-done.1 = bf16[96,96]{1,0:T(8,128)(2,1)S(1)} collective-permute-done((bf16[96,96]{1,0:T(8,128)(2,1)S(1)}, bf16[96,96]{1,0:T(8,128)(2,1)S(1)}, u32[]{:S(2)}, u32[]{:S(2)}) %collective-permute-start.1) | collective-permute-done | bytes 18464 | tf_op jit(solution)/shard_map/ppermute | solution.py:14
  175.1 1.8 multiply_subtract_fusion
  183.7 1.9 collective-permute-start.5
  187.9 4.6 %collective-permute-start.9 = (bf16[96,96]{1,0:T(8,128)(2,1)S(1)}, bf16[96,96]{1,0:T(8,128)(2,1)S(1)}, u32[]{:S(2)}, u32[]{:S(2)}) collective-permute-start(bf16[96,96]{1,0:T(8,128)(2,1)S(1)} %divide_convert_fusion), channel_id=1, source_target_pairs={{0,32},{32,64},{64,96},{96,128},{128,160},{160,192},{192,224},{224... | collective-permute-start | bytes 55304 | tf_op jit(solution)/shard_map/ppermute | solution.py:14
  192.9 16.9 %collective-permute-done.5 = bf16[1536,96]{0,1:T(8,128)(2,1)S(1)} collective-permute-done((bf16[1536,96]{0,1:T(8,128)(2,1)S(1)}, bf16[1536,96]{0,1:T(8,128)(2,1)S(1)}, u32[]{:S(2)}, u32[]{:S(2)}) %collective-permute-start.5) | collective-permute-done | bytes 294944 | tf_op jit(solution)/shard_map/ppermute | solution.py:14
  210.2 46.4 %while.21 = (s32[]{:T(128)}, f32[6,16,96,4,4]{2,1,4,3,0:T(8,128)S(1)}, s32[6]{0:T(128)S(1)}, bf16[96,16,96]{0,2,1:T(8,128)(2,1)S(1)}, bf16[96,16,96]{2,0,1:T(8,1...) while((s32[]{:T(128)}, ...), condition=%wide.region_10.11_spmd, body=%wide.region_9.10_spmd.sunk | while | flops 202899456 | bytes 7538859 | solution.py:82
  215.1 2.0 fusion.177
  221.0 1.8 fusion.176
  222.8 2.0 fusion.177
  230.5 2.0 fusion.177
  238.3 2.0 fusion.177
  246.0 2.0 fusion.177
  253.8 2.0 fusion.177
  258.4 15.9 %collective-permute-start.8 = (bf16[96,1536]{1,0:T(8,128)(2,1)S(1)}, bf16[96,1536]{1,0:T(8,128)(2,1)S(1)}, u32[]{:S(2)}, u32[]{:S(2)}) collective-permute-start(bf16[96,1536]{1,0:T(8,128)(2,1)S(1)} %copy.72), channel_id=1, source_target_pairs={{0,32},{32,64},{64,96},{96,128},{128,160},{160,192},{192,224},{224... | collective-permute-start | bytes 884744 | tf_op jit(solution)/shard_map/ppermute | solution.py:14
  276.2 1.9 collective-permute-start.6
  (150 shorter events, 84.4 us)
Async XLA Ops:
  0.6 1.0 copy-start
  0.6 23.3 %copy-start.10 = (f32[2,2]{1,0:T(2,128)S(1)}, f32[2,2]{1,0:T(2,128)}, u32[]{:S(2)}) copy-start(f32[2,2]{1,0:T(2,128)} %param.18) | copy-start | bytes 52
  0.7 23.5 %copy-start.9 = (bf16[1,1,2,256]{3,2,1,0:T(2,128)(2,1)S(1)}, bf16[1,1,2,256]{3,2,1,0:T(2,128)(2,1)}, u32[]{:S(2)}) copy-start(bf16[1,1,2,256]{3,2,1,0:T(2,128)(2,1)} %param.17) | copy-start | bytes 3076
  0.7 23.6 %copy-start.1 = (bf16[1,1,96,1536]{3,2,1,0:T(8,128)(2,1)S(1)}, bf16[1,1,96,1536]{3,2,1,0:T(8,128)(2,1)}, u32[]{:S(2)}) copy-start(bf16[1,1,96,1536]{3,2,1,0:T(8,128)(2,1)} %param.16) | copy-start | bytes 884740
  0.7 23.6 %copy-start.8 = (bf16[1,1,96,96]{3,2,1,0:T(8,128)(2,1)S(1)}, bf16[1,1,96,96]{3,2,1,0:T(8,128)(2,1)}, u32[]{:S(2)}) copy-start(bf16[1,1,96,96]{3,2,1,0:T(8,128)(2,1)} %param.15) | copy-start | bytes 55300
  3.0 22.1 %copy-start.11 = (s32[4]{0:T(128)S(1)}, s32[4]{0:T(128)}, u32[]{:S(2)}) copy-start(s32[4]{0:T(128)} %param.19) | copy-start | bytes 52
  3.0 45.3 %collective-permute-start = (bf16[1536,96]{0,1:T(8,128)(2,1)S(1)}, bf16[1536,96]{0,1:T(8,128)(2,1)S(1)}, u32[]{:S(2)}, u32[]{:S(2)}) collective-permute-start(bf16[1536,96]{0,1:T(8,128)(2,1)S(1)} %copy.49), channel_id=1, source_target_pairs={{0,31},{1,0},{2,1},{3,2},{4,3},{5,4},{6,5},{7,6},{8,7},{9,8},{10,9... | collective-permute-start | bytes 884744 | tf_op jit(solution)/shard_map/ppermute | solution.py:14
  55.9 6.0 %copy-start.2 = (bf16[1,1,96,1536]{3,2,1,0:T(8,128)(2,1)S(1)}, bf16[1,1,96,1536]{3,2,1,0:T(8,128)(2,1)}, u32[]{:S(2)}) copy-start(bf16[1,1,96,1536]{3,2,1,0:T(8,128)(2,1)} %param.14) | copy-start | bytes 884740
  58.7 32.1 %collective-permute-start.2 = (bf16[1536,96]{0,1:T(8,128)(2,1)}, bf16[1536,96]{0,1:T(8,128)(2,1)}, u32[]{:S(2)}, u32[]{:S(2)}) collective-permute-start(bf16[1536,96]{0,1:T(8,128)(2,1)} %get-tuple-element.171), channel_id=1, source_target_pairs={{0,1},{1,2},{2,3},{3,4},{4,5},{5,6},{6,7},{7,8},{8,9},{9,10},{10,1... | collective-permute-start | bytes 884744 | tf_op jit(solution)/shard_map/ppermute | solution.py:14
  66.2 32.6 %copy-start.4 = (bf16[2,4,4,4,4]{4,3,1,2,0:T(4,128)(2,1)S(1)}, bf16[2,4,4,4,4]{4,3,1,2,0:T(4,128)(2,1)}, u32[]{:S(2)}) copy-start(bf16[2,4,4,4,4]{4,3,1,2,0:T(4,128)(2,1)} %copy.60) | copy-start | bytes 3076
  66.2 32.6 %copy-start.6 = (bf16[2,4,4,4,4]{4,3,0,1,2:T(4,128)(2,1)S(1)}, bf16[2,4,4,4,4]{4,3,0,1,2:T(4,128)(2,1)}, u32[]{:S(2)}) copy-start(bf16[2,4,4,4,4]{4,3,0,1,2:T(4,128)(2,1)} %copy.61) | copy-start | bytes 3076
  93.6 55.3 %collective-permute-start.3 = (bf16[96,96]{1,0:T(8,128)(2,1)S(1)}, bf16[96,96]{1,0:T(8,128)(2,1)S(1)}, u32[]{:S(2)}, u32[]{:S(2)}) collective-permute-start(bf16[96,96]{1,0:T(8,128)(2,1)S(1)} %divide_convert_fusion.2), channel_id=1, source_target_pairs={{0,32},{32,64},{64,96},{96,128},{128,160},{160,192},{192,224},{224... | collective-permute-start | bytes 55304 | tf_op jit(solution)/shard_map/ppermute | solution.py:14
  146.8 5.4 %copy-start.3 = (f32[96,96]{1,0:T(8,128)S(1)}, f32[96,96]{1,0:T(8,128)}, u32[]{:S(2)}) copy-start(f32[96,96]{1,0:T(8,128)} %get-tuple-element.170) | copy-start | bytes 110596
  147.0 22.5 %collective-permute-start.7 = (bf16[96,1536]{1,0:T(8,128)(2,1)S(1)}, bf16[96,1536]{1,0:T(8,128)(2,1)}, u32[]{:S(2)}, u32[]{:S(2)}) collective-permute-start(bf16[96,1536]{1,0:T(8,128)(2,1)S(1)} %copy.100), channel_id=1, source_target_pairs={{0,32},{32,64},{64,96},{96,128},{128,160},{160,192},{192,224},{224... | collective-permute-start | bytes 884744 | tf_op jit(solution)/shard_map/ppermute | solution.py:14
  150.3 20.6 %collective-permute-start.4 = (bf16[1536,96]{0,1:T(8,128)(2,1)}, bf16[1536,96]{0,1:T(8,128)(2,1)}, u32[]{:S(2)}, u32[]{:S(2)}) collective-permute-start(bf16[1536,96]{0,1:T(8,128)(2,1)} %copy.51), channel_id=1, source_target_pairs={{0,31},{1,0},{2,1},{3,2},{4,3},{5,4},{6,5},{7,6},{8,7},{9,8},{10,9... | collective-permute-start | bytes 884744 | tf_op jit(solution)/shard_map/ppermute | solution.py:14
  152.2 16.5 %collective-permute-start.1 = (bf16[96,96]{1,0:T(8,128)(2,1)S(1)}, bf16[96,96]{1,0:T(8,128)(2,1)S(1)}, u32[]{:S(2)}, u32[]{:S(2)}) collective-permute-start(bf16[96,96]{1,0:T(8,128)(2,1)S(1)} %divide_convert_fusion.3), channel_id=1, source_target_pairs={{0,32},{32,64},{64,96},{96,128},{128,160},{160,192},{192,224},{224... | collective-permute-start | bytes 55304 | tf_op jit(solution)/shard_map/ppermute | solution.py:14
  183.7 26.1 %collective-permute-start.5 = (bf16[1536,96]{0,1:T(8,128)(2,1)S(1)}, bf16[1536,96]{0,1:T(8,128)(2,1)S(1)}, u32[]{:S(2)}, u32[]{:S(2)}) collective-permute-start(bf16[1536,96]{0,1:T(8,128)(2,1)S(1)} %get-tuple-element.175), channel_id=1, source_target_pairs={{0,1},{1,2},{2,3},{3,4},{4,5},{5,6},{6,7},{7,8},{8,9},{9,10},{10,1... | collective-permute-start | bytes 884744 | tf_op jit(solution)/shard_map/ppermute | solution.py:14
  187.0 23.2 %copy-start.5 = (bf16[2,4,4,4,4]{4,3,1,2,0:T(4,128)(2,1)S(1)}, bf16[2,4,4,4,4]{4,3,1,2,0:T(4,128)(2,1)}, u32[]{:S(2)}) copy-start(bf16[2,4,4,4,4]{4,3,1,2,0:T(4,128)(2,1)} %copy.60) | copy-start | bytes 3076
  187.0 23.3 %copy-start.7 = (bf16[2,4,4,4,4]{4,3,0,1,2:T(4,128)(2,1)S(1)}, bf16[2,4,4,4,4]{4,3,0,1,2:T(4,128)(2,1)}, u32[]{:S(2)}) copy-start(bf16[2,4,4,4,4]{4,3,0,1,2:T(4,128)(2,1)} %copy.61) | copy-start | bytes 3076
  187.9 90.2 %collective-permute-start.9 = (bf16[96,96]{1,0:T(8,128)(2,1)S(1)}, bf16[96,96]{1,0:T(8,128)(2,1)S(1)}, u32[]{:S(2)}, u32[]{:S(2)}) collective-permute-start(bf16[96,96]{1,0:T(8,128)(2,1)S(1)} %divide_convert_fusion), channel_id=1, source_target_pairs={{0,32},{32,64},{64,96},{96,128},{128,160},{160,192},{192,224},{224... | collective-permute-start | bytes 55304 | tf_op jit(solution)/shard_map/ppermute | solution.py:14
  258.4 20.8 %collective-permute-start.8 = (bf16[96,1536]{1,0:T(8,128)(2,1)S(1)}, bf16[96,1536]{1,0:T(8,128)(2,1)S(1)}, u32[]{:S(2)}, u32[]{:S(2)}) collective-permute-start(bf16[96,1536]{1,0:T(8,128)(2,1)S(1)} %copy.72), channel_id=1, source_target_pairs={{0,32},{32,64},{64,96},{96,128},{128,160},{160,192},{192,224},{224... | collective-permute-start | bytes 884744 | tf_op jit(solution)/shard_map/ppermute | solution.py:14
  276.2 3.1 %collective-permute-start.6 = (bf16[96,96]{1,0:T(8,128)(2,1)S(1)}, bf16[96,96]{1,0:T(8,128)(2,1)S(1)}, u32[]{:S(2)}, u32[]{:S(2)}) collective-permute-start(bf16[96,96]{1,0:T(8,128)(2,1)S(1)} %divide_convert_fusion.1), channel_id=1, source_target_pairs={{0,32},{32,64},{64,96},{96,128},{128,160},{160,192},{192,224},{224... | collective-permute-start | bytes 55304 | tf_op jit(solution)/shard_map/ppermute | solution.py:14
where the time goes:
time: 285 us; the launch traced here: 281 us
  matrix products  90.2 us (32%)
  waiting for transfers between devices  78.6 us (28%)
  starting transfers between devices  56.8 us (20%)
  loops' own time  23.8 us (8%)
  local copies, waits for them, and re-layouts  20 us (7%)
  between operations  6.92 us (2%)
  other arithmetic  4.9 us (2%)
    ppermute x10, waiting for transfers between devices, passed_along(): lax.ppermute(shard, axis, [(i, (i + by) % peers) for i in range(peers)])  78.6 us
    ppermute x10, starting transfers between devices, passed_along(): lax.ppermute(shard, axis, [(i, (i + by) % peers) for i in range(peers)])  56.8 us
    dot_general x12, matrix products, one_block(): jnp.einsum('uefjsgc,sehkf->ughckj', second, bra, preferred_element_type=j...  24.3 us
    another operation x2, loops' own time, per_device(): pieces = lax.map(one_block, starts)  23.8 us
    dot_general x12, matrix products, one_block(): jnp.einsum('uaebfj,sagcb->uefjsgc', first, ket_sites, preferred_element_t...  21.5 us
    dot_general x12, matrix products, one_block(): jnp.einsum('ughi,ughckj->jick', up_half, third, preferred_element_type=jn...  10.6 us
    dot_general x12, matrix products, polar_factor(): jnp.dot(iterate, gram, precision=lax.Precision.HIGHEST)  10.5 us
    dot_general x12, matrix products, polar_factor(): gram = jnp.dot(iterate.T, iterate, precision=lax.Precision.HIGHEST)  8.64 us
  transfers between devices with their start and end apart: 10, of which 5 were waited for; matrix products, arithmetic and copies ran while one was open for 31% of the time, Pallas kernels for 0%

commit v1 on v0

v1 whole, which is shorter than its diff:
```python
import jax
import jax.numpy as jnp
from jax import lax
from jax.experimental import pallas as pl
from jax.experimental.pallas import tpu as pltpu
from jax.sharding import PartitionSpec as P

NS_ITERS = 6
STEPS = 2
MESH = pl.DeviceIdType.MESH
CHI = 96
B = 16
L = 128
F32 = jnp.float32
BF = jnp.bfloat16


def nt(a, b):
    return lax.dot_general(a, b, (((1,), (1,)), ((), ())), preferred_element_type=F32)


def nn(a, b):
    return jnp.dot(a, b, preferred_element_type=F32)


def split(x):
    hi = x.astype(BF)
    return hi, (x - hi.astype(F32)).astype(BF)


def product(a, b):
    a_hi, a_lo = split(a)
    b_hi, b_lo = split(b)
    return nn(
        jnp.concatenate([a_hi, a_lo], axis=1), jnp.concatenate([b_hi, b_hi], axis=0)
    ) + nn(a_hi, b_lo)


def eye():
    row = lax.broadcasted_iota(jnp.int32, (L, L), 0)
    col = lax.broadcasted_iota(jnp.int32, (L, L), 1)
    return jnp.where((row == col) & (row < CHI), 1.0, 0.0).astype(F32)


def polar_right(grams):
    one = eye()
    scales = [1.0 / (jnp.sum(g * one) + 1e-06) for g in grams]
    ss = [g * s for g, s in zip(grams, scales)]
    ps = [1.5 * one - 0.5 * s for s in ss]
    ms = list(ps)
    for _ in range(NS_ITERS - 1):
        vs = [product(s, p) for s, p in zip(ss, ps)]
        ss = [product(v, p) for v, p in zip(vs, ps)]
        ps = [1.5 * one - 0.5 * s for s in ss]
        ms = [product(m, p) for m, p in zip(ms, ps)]
    return [m * jnp.sqrt(s) for m, s in zip(ms, scales)]


def unit_corner(x):
    return (x * lax.rsqrt(jnp.sum(x * x) * (1.0 / (CHI * CHI)) + 1e-06)).astype(BF)


def transposed_edge(edge_ref, out_ref):
    for chunk in range(4):
        lanes = edge_ref[:, chunk * 384 : (chunk + 1) * 384]
        lanes = jnp.concatenate([lanes, jnp.zeros((L - CHI, 384), BF)], axis=0)
        turned = lanes.T
        for i in range(4):
            d = chunk * 4 + i
            out_ref[d * L : d * L + CHI, :] = turned[i * CHI : (i + 1) * CHI, :]
            out_ref[d * L + CHI : (d + 1) * L, :] = jnp.zeros((L - CHI, L), BF)


def double_layer(ket_ref, gate_ref, quench_ref, own_index, out_ref):
    n = lax.broadcasted_iota(jnp.int32, (256, 256), 0)
    m = lax.broadcasted_iota(jnp.int32, (256, 256), 1)
    f4 = lambda x, k: (x >> (6 - 2 * k)) & 3
    ket_mask = (f4(n, 2) == f4(m, 1)) & (f4(n, 0) == f4(m, 2))
    bra_mask = (f4(n, 3) == f4(m, 1)) & (f4(n, 1) == f4(m, 2))
    ket_spread = ((f4(n, 0) == f4(m, 2)) & (f4(n, 3) == f4(m, 0))).astype(F32).astype(BF)
    bra_spread = ((f4(n, 0) == f4(m, 3)) & (f4(n, 3) == f4(m, 1))).astype(F32).astype(BF)
    chosen = quench_ref[0] == own_index
    for i in range(1, 4):
        chosen = chosen | (quench_ref[i] == own_index)
    kets = [ket_ref[0, 0, s : s + 1, :].astype(F32) for s in range(2)]
    total = jnp.zeros((256, 256), F32)
    for s in range(2):
        bra = jnp.zeros((1, 256), F32)
        for t in range(2):
            gram = gate_ref[0, s] * gate_ref[0, t] + gate_ref[1, s] * gate_ref[1, t]
            weight = jnp.where(chosen, gram, 1.0 if s == t else 0.0)
            bra = bra + weight * kets[t]
        bra = bra.astype(BF).astype(F32)
        ket_part = nn(jnp.where(ket_mask, kets[s], 0.0).astype(BF), ket_spread)
        bra_part = nn(jnp.where(bra_mask, bra, 0.0).astype(BF), bra_spread)
        total = total + ket_part * bra_part
    out_ref[...] = total.astype(BF)


def kernel(
    c_up_in, e_up_in, e_left_in, c_low_in, e_low_in, ket_ref, gate_ref, quench_ref,
    c_up_out, e_out, c_low_out,
    own_up, own_low, near_up, near_low, west_nat, c_in,
    et_ll, et_lu, et_ul, et_uu, cpad, c_send, c_recv, w_ref, west, west_recv, west_send,
    gt_b, lt_b, ut_b, gt_a, lt_a, ut_a, inter, pup, pt, fs, t_ref, e_fin, c_fin,
    lsem, ssem, rsem,
):
    gx, gy = lax.axis_index("gx"), lax.axis_index("gy")
    ncol, nrow = lax.axis_size("gx"), lax.axis_size("gy")
    north = (gx, lax.rem(gy + nrow - 1, nrow))
    south = (gx, lax.rem(gy + 1, nrow))
    east = (lax.rem(gx + 1, ncol), gy)
    before = (lax.rem(gx + ncol - 1, ncol), gy)
    barrier = pltpu.get_barrier_semaphore()
    for peer in (north, south, east, before):
        pl.semaphore_signal(barrier, inc=1, device_id=peer, device_id_type=MESH)

    local = [
        pltpu.make_async_copy(src.at[0, 0], dst, lsem.at[i])
        for i, (src, dst) in enumerate((
            (e_up_in, own_up), (e_low_in, own_low), (e_left_in, west_nat),
            (c_up_in, c_in.at[0]), (c_low_in, c_in.at[1]),
        ))
    ]
    for copy in local:
        copy.start()
    pl.semaphore_wait(barrier, 4)

    def remote(src, dst, i, peer):
        return pltpu.make_async_remote_copy(
            src_ref=src, dst_ref=dst, send_sem=ssem.at[i], recv_sem=rsem.at[i],
            device_id=peer, device_id_type=MESH,
        )

    first_sends = [
        remote(e_up_in.at[0, 0], near_up, 0, north),
        remote(e_low_in.at[0, 0], near_low, 1, south),
        remote(c_up_in.at[0, 0], c_in.at[2], 2, north),
        remote(c_low_in.at[0, 0], c_in.at[3], 3, south),
    ]
    for copy in first_sends:
        copy.start()

    double_layer(ket_ref, gate_ref, quench_ref, gx * nrow + gy, w_ref)
    for copy in local:
        copy.wait()
    transposed_edge(own_up, et_uu)
    transposed_edge(own_low, et_ll)
    for l in range(B):
        inter[pl.ds(l, CHI, stride=B), :] = jnp.concatenate(
            [west_nat[:, l * CHI : (l + 1) * CHI].astype(F32), jnp.zeros((CHI, L - CHI), F32)], axis=1
        )
    west[...] = inter[...].astype(BF)

    for copy in first_sends:
        copy.wait_recv()
    for slot, place in enumerate((1, 2, 3, 0)):
        cpad[slot] = jnp.zeros((L, L), BF)
        cpad[slot, 0:CHI, :] = jnp.concatenate([c_in[place], jnp.zeros((CHI, L - CHI), BF)], axis=1)
    transposed_edge(near_up, et_lu)
    transposed_edge(near_low, et_ul)

    for step in range(STEPS):
        corners = cpad if step == 0 else c_recv
        if step > 0:
            remote(c_send, c_recv, 4, east).wait_recv()
        cuts = ((et_ll, et_lu, 0, 1, gt_b, lt_b, ut_b), (et_ul, et_uu, 2, 3, gt_a, lt_a, ut_a))
        grams, rows_low, rows_up = [], [], []
        for et_low, et_up, i_low, i_up, gt, lt, ut in cuts:
            for piece in range(8):
                rows = slice(piece * 256, (piece + 1) * 256)
                low = nt(et_low[rows, :], corners[i_low])
                up = nt(et_up[rows, :], corners[i_up])
                gt[rows, :] = (low + up).astype(BF)
                lt[rows, :] = low.astype(BF)
                ut[rows, :] = up.astype(BF)
            total = jnp.zeros((L, 3 * L), F32)
            for d in range(B):
                rows = slice(d * L, (d + 1) * L)
                right = jnp.concatenate([gt[rows, :], lt[rows, :], ut[rows, :]], axis=0)
                total = total + nt(gt[rows, :], right)
            grams.append(total[:, 0:L])
            rows_low.append(total[:, L : 2 * L])
            rows_up.append(total[:, 2 * L : 3 * L])
        for up in range(B):
            rows = slice(up * L, (up + 1) * L)
            value = nt(corners[2], et_ul[rows, :]) + nt(corners[3], et_uu[rows, :])
            inter[pl.ds(up, CHI, stride=B), :] = value[0:CHI, :]
        m_b, m_a = polar_right(grams)
        new_low_b = unit_corner(product(m_b, rows_low[0]))
        new_up_a = unit_corner(product(m_a, rows_up[1]))
        if step < STEPS - 1:
            c_send[0] = new_low_b
            c_send[1] = unit_corner(product(m_b, rows_up[0]))
            c_send[2] = unit_corner(product(m_a, rows_low[1]))
            c_send[3] = new_up_a
            corner_sends = [remote(c_send, c_recv, 4, east)]
        else:
            c_fin[0] = new_up_a[0:CHI, 0:CHI]
            c_fin[1] = new_low_b[0:CHI, 0:CHI]
            corner_sends = [
                remote(c_fin.at[0], c_up_out.at[0, 0], 5, east),
                remote(c_fin.at[1], c_low_out.at[0, 0], 6, east),
            ]
        for copy in corner_sends:
            copy.start()

        m_rows = jnp.concatenate(list(split(m_b)), axis=0)
        for d in range(B):
            rows = slice(d * L, (d + 1) * L)
            both = nn(m_rows, gt_b[rows, :])
            pt[rows, :] = (both[0:L] + both[L : 2 * L]).astype(BF)
        m_rows = jnp.concatenate(list(split(m_a)), axis=0)
        for piece in range(6):
            rows = slice(piece * 256, (piece + 1) * 256)
            both = nt(m_rows, inter[rows, :].astype(BF))
            pup[:, rows] = (both[0:CHI] + both[L : L + CHI]).astype(BF)

        if step > 0:
            remote(west_send, west_recv, 7, east).wait_recv()
        left = west if step == 0 else west_recv

        def block(i, carry):
            base = pl.multiple_of(i * 256, 256)
            rows = left[pl.ds(base, 256), :]
            for pair in range(8):
                out = nt(rows, pt[pair * 256 : (pair + 1) * 256, :]).astype(BF)
                fs[2 * pair] = out[:, 0:L]
                fs[2 * pair + 1] = out[:, L : 2 * L]
            for pair in range(8):
                cols = [
                    jnp.concatenate([fs[d, u * B : (u + 1) * B, :] for d in range(B)], axis=0)
                    for u in (2 * pair, 2 * pair + 1)
                ]
                out = nn(w_ref[...], jnp.concatenate(cols, axis=1)).astype(BF)
                for half in range(2):
                    at = pl.ds(pl.multiple_of(base + (2 * pair + half) * B, B), B)
                    for r in range(B):
                        t_ref[r // 2, at, (r % 2) * L : (r % 2 + 1) * L] = out[
                            r * B : (r + 1) * B, half * L : (half + 1) * L
                        ]
            return carry

        lax.fori_loop(0, 6, block, 0)

        square = jnp.zeros((CHI, CHI), F32)
        blocks = []
        for pair in range(8):
            out = nn(pup[...], t_ref[pair])
            for half in range(2):
                value = out[:, half * L : half * L + CHI]
                square = square + value * value
                r = 2 * pair + half
                if step < STEPS - 1:
                    inter[pl.ds(r, CHI, stride=B), :] = jnp.concatenate(
                        [value, jnp.zeros((CHI, L - CHI), F32)], axis=1
                    )
                else:
                    blocks.append(value)
        scale = lax.rsqrt(jnp.sum(square) * (1.0 / (CHI * CHI * B)) + 1e-06)
        if step < STEPS - 1:
            west_send[...] = (inter[...] * scale).astype(BF)
            edge_send = remote(west_send, west_recv, 7, east)
        else:
            e_fin[...] = jnp.concatenate([(v * scale).astype(BF) for v in blocks], axis=1)
            edge_send = remote(e_fin, e_out.at[0, 0], 8, east)
        edge_send.start()
        if step == STEPS - 1:
            for copy in corner_sends + [edge_send]:
                copy.wait_recv()
            for copy in corner_sends + [edge_send] + first_sends:
                copy.wait_send()
            remote(c_send, c_recv, 4, east).wait_send()
            remote(west_send, west_recv, 7, east).wait_send()


def per_device(c_upper, edge_upper, edge_left, c_lower, edge_lower, site_ket, time_gate, quench_sites):
    hbm = pl.BlockSpec(memory_space=pl.ANY)
    vmem = pl.BlockSpec(memory_space=pltpu.VMEM)
    smem = pl.BlockSpec(memory_space=pltpu.SMEM)
    corner = jax.ShapeDtypeStruct((1, 1, CHI, CHI), BF)
    edge = jax.ShapeDtypeStruct((1, 1, CHI, B * CHI), BF)
    natural = pltpu.VMEM((CHI, B * CHI), BF)
    tall = pltpu.VMEM((B * L, L), BF)
    inner = pltpu.VMEM((CHI * B, L), BF)
    four = pltpu.VMEM((4, L, L), BF)
    return pl.pallas_call(
        kernel,
        out_shape=(corner, edge, corner),
        in_specs=[hbm] * 5 + [vmem, smem, smem],
        out_specs=(hbm,) * 3,
        scratch_shapes=[
            natural, natural, natural, natural, natural, pltpu.VMEM((4, CHI, CHI), BF),
            tall, tall, tall, tall, four, four, four, pltpu.VMEM((256, 256), BF), inner, inner, inner,
            tall, tall, tall, tall, tall, tall, pltpu.VMEM((CHI * B, L), F32),
            pltpu.VMEM((CHI, CHI * B), BF), tall, pltpu.VMEM((B, 256, L), BF),
            pltpu.VMEM((8, CHI * B, 2 * L), BF), natural, pltpu.VMEM((2, CHI, CHI), BF),
            pltpu.SemaphoreType.DMA((5,)), pltpu.SemaphoreType.DMA((9,)), pltpu.SemaphoreType.DMA((9,)),
        ],
        compiler_params=pltpu.CompilerParams(
            collective_id=0, has_side_effects=True, vmem_limit_bytes=63 * 1024 * 1024
        ),
        name="left_move",
    )(c_upper, edge_upper, edge_left, c_lower, edge_lower, site_ket, time_gate, quench_sites)


def solution(mesh):
    site = P("gx", "gy", None, None)
    return jax.shard_map(
        per_device,
        mesh=mesh,
        in_specs=(site,) * 6 + (P(), P()),
        out_specs=(site,) * 3,
        check_vma=False,
    )
```

time: 285 us -> 88 us (0.31); the launches traced: 281 us -> 87.8 us
  matrix products: 90.2 us -> 0 us
  Pallas kernels: 0 us -> 83.5 us
  waiting for transfers between devices: 78.6 us -> 0 us
  starting transfers between devices: 56.8 us -> 0 us
  loops' own time: 23.8 us -> 0 us
  local copies, waits for them, and re-layouts: 20 us -> 3.66 us
  between operations: 6.92 us -> 0.64 us
  other arithmetic: 4.9 us -> 0 us
    dot_general x82 -> x0, matrix products: 90.2 us -> none  [the longest x12 24.3 us: one_block(): jnp.einsum('uefjsgc,sehkf->ughckj', second, bra, preferred_element_type=j...]
    pallas_call x0 -> x1, Pallas kernels: none -> 83.5 us  [per_device(): pl.pallas_call(kernel, out_shape=(corner, edge, corner), in_specs=[hbm] *...]
    ppermute x10 -> x0, waiting for transfers between devices: 78.6 us -> none  [passed_along(): lax.ppermute(shard, axis, [(i, (i + by) % peers) for i in range(peers)])]
    ppermute x10 -> x0, starting transfers between devices: 56.8 us -> none  [passed_along(): lax.ppermute(shard, axis, [(i, (i + by) % peers) for i in range(peers)])]
    another operation x2 -> x0, loops' own time: 23.8 us -> none  [per_device(): pieces = lax.map(one_block, starts)]
    dynamic_slice x12 -> x0, local copies, waits for them, and re-layouts: 7.04 us -> none  [per_device(): pieces = lax.map(one_block, starts)]
    reduce_sum x4 -> x0, other arithmetic: 4.08 us -> none  [the longest x2 2.47 us: polar_factor(): scale = jnp.sqrt(jnp.sum(matrix * matrix) + 1e-06)]
    reshape x9 -> x0, local copies, waits for them, and re-layouts: 3.86 us -> none  [the longest x4 1.55 us: per_device(): jnp.dot(corner_up, north_edge, preferred_element_type=jnp.float32)]
  transfers between devices with their start and end apart: 10 -> 0, of which waited for: 5 -> 0; matrix products, arithmetic and copies ran while one was open for 31% -> 0% of each run, Pallas kernels for 0% -> 0%
where the time goes in v1:
time: 88 us; the launch traced here: 87.8 us
  Pallas kernels  83.5 us (95%)
  local copies, waits for them, and re-layouts  3.66 us (4%)
    pallas_call x1, Pallas kernels, per_device(): pl.pallas_call(kernel, out_shape=(corner, edge, corner), in_specs=[hbm] *...  83.5 us
    unnamed x5, local copies, waits for them, and re-layouts  3.66 us

profile of v1, /device:TPU:1, one launch (start us, length us, event | category | flops | bytes accessed | tf_op | source)
XLA Modules:
  0.0 87.8 jit_solution(8292830318224919503)
XLA Ops:
  0.6 83.5 %left_move.1 = (bf16[1,1,96,96]{3,2,1,0:T(8,128)(2,1)}, bf16[1,1,96,1536]{3,2,1,0:T(8,128)(2,1)}, bf16[1,1,96,96]{3,2,1,0:T(8,128)(2,1)}) custom-call(bf16[1,1,96,96]{3,2,1,0:T(8,128)(2,1)} %c_up_in.1, bf16[1,1,96,1536]{3,2,1,0:T(8,128)(2,1)} %e_up_in.1, bf16[1,1,96,1536]{3,2,1,0:T(8,128)(2,1)} %e_left_in.1, bf16[1,1,96,96]{3,2,1,0:T(8,128)(2,1)} %c_low_in.1, ...), custom_call_target="tpu_custom_call" | custom-call | tf_op jit(solution)/shard_map/left_move/pallas_call | solution.py:287
  84.1 1.3 %copy.14 = bf16[1,1,96,96]{3,2,1,0:T(8,128)(2,1)} copy(bf16[1,1,96,96]{3,2,1,0:T(8,128)(2,1)} %get-tuple-element.6) | data formatting | bytes 36864
  85.4 0.0 copy-start
  85.4 1.7 %copy.15 = bf16[1,1,96,1536]{3,2,1,0:T(8,128)(2,1)} copy(bf16[1,1,96,1536]{3,2,1,0:T(8,128)(2,1)} %get-tuple-element.7) | data formatting | bytes 589824
  87.1 0.0 copy-done
  87.1 0.6 copy.16
Async XLA Ops:
  85.4 1.7 %copy-start = (bf16[1,1,96,96]{3,2,1,0:T(8,128)(2,1)S(1)}, bf16[1,1,96,96]{3,2,1,0:T(8,128)(2,1)}, u32[]{:S(2)}) copy-start(bf16[1,1,96,96]{3,2,1,0:T(8,128)(2,1)} %get-tuple-element.8) | copy-start | bytes 55300

commit v2 on v1

--- a/solution.py
+++ b/solution.py
@@ -10,6 +10,8 @@
 MESH = pl.DeviceIdType.MESH
 CHI = 96
 B = 16
+HALF = 16
+CHUNKS = 12
 L = 128
 F32 = jnp.float32
 BF = jnp.bfloat16
@@ -103,7 +105,7 @@
     own_up, own_low, near_up, near_low, west_nat, c_in,
     et_ll, et_lu, et_ul, et_uu, cpad, c_send, c_recv, w_ref, west, west_recv, west_send,
     gt_b, lt_b, ut_b, gt_a, lt_a, ut_a, inter, pup, pt, fs, t_ref, e_fin, c_fin,
-    lsem, ssem, rsem,
+    hop, lsem, ssem, rsem, psem, hsem,
 ):
     gx, gy = lax.axis_index("gx"), lax.axis_index("gy")
     ncol, nrow = lax.axis_size("gx"), lax.axis_size("gy")
@@ -111,9 +113,31 @@
     south = (gx, lax.rem(gy + 1, nrow))
     east = (lax.rem(gx + 1, ncol), gy)
     before = (lax.rem(gx + ncol - 1, ncol), gy)
+    half, place = gy // HALF, lax.rem(gy, HALF)
+    spread = nrow == 2 * HALF
+    first, last = place == 0, place == HALF - 1
+    helper = (place >= 2) & (place < 2 + CHUNKS)
     barrier = pltpu.get_barrier_semaphore()
+
+    def greet(peer):
+        pl.semaphore_signal(barrier, inc=1, device_id=peer, device_id_type=MESH)
+
     for peer in (north, south, east, before):
-        pl.semaphore_signal(barrier, inc=1, device_id=peer, device_id_type=MESH)
+        greet(peer)
+    greeted = 4
+    if spread:
+        @pl.when(first | last)
+        def _():
+            for c in range(CHUNKS):
+                greet((gx, 2 + c))
+                greet((gx, HALF + 2 + c))
+
+        @pl.when(helper)
+        def _():
+            for row in (0, HALF - 1, HALF, 2 * HALF - 1):
+                greet((gx, row))
+
+        greeted = 4 + jnp.where(helper, 4, 0) + jnp.where(first | last, 2 * CHUNKS, 0)
 
     local = [
         pltpu.make_async_copy(src.at[0, 0], dst, lsem.at[i])
@@ -124,7 +148,7 @@
     ]
     for copy in local:
         copy.start()
-    pl.semaphore_wait(barrier, 4)
+    pl.semaphore_wait(barrier, greeted)
 
     def remote(src, dst, i, peer):
         return pltpu.make_async_remote_copy(
@@ -138,8 +162,52 @@
         remote(c_up_in.at[0, 0], c_in.at[2], 2, north),
         remote(c_low_in.at[0, 0], c_in.at[3], 3, south),
     ]
-    for copy in first_sends:
-        copy.start()
+    def relay(src, dst, send, recv, peer):
+        return pltpu.make_async_remote_copy(
+            src_ref=src, dst_ref=dst, send_sem=psem.at[send], recv_sem=recv,
+            device_id=peer, device_id_type=MESH,
+        )
+
+    def chunk_sends(edge_in, slot):
+        return [
+            relay(edge_in.at[0, 0, :, pl.ds(c * L, L)], hop.at[slot], c, hsem.at[slot], (gx, half * HALF + 2 + c))
+            for c in range(CHUNKS)
+        ]
+
+    lanes = pl.ds(pl.multiple_of((place - 2) * L, L), L)
+    forwards = [
+        relay(hop.at[0], near_up.at[:, lanes], 0, rsem.at[0], (gx, (1 - half) * HALF + HALF - 1)),
+        relay(hop.at[1], near_low.at[:, lanes], 1, rsem.at[1], (gx, (1 - half) * HALF)),
+    ]
+    if spread:
+        @pl.when(first)
+        def _():
+            for copy in chunk_sends(e_up_in, 0):
+                copy.start()
+
+        @pl.when(last)
+        def _():
+            for copy in chunk_sends(e_low_in, 1):
+                copy.start()
+
+        @pl.when(jnp.logical_not(first))
+        def _():
+            first_sends[0].start()
+
+        @pl.when(jnp.logical_not(last))
+        def _():
+            first_sends[1].start()
+    else:
+        first_sends[0].start()
+        first_sends[1].start()
+    first_sends[2].start()
+    first_sends[3].start()
+    if spread:
+        @pl.when(helper)
+        def _():
+            for slot in (0, 1):
+                relay(hop.at[slot], hop.at[slot], slot, hsem.at[slot], north).wait_recv()
+                forwards[slot].start()
 
     double_layer(ket_ref, gate_ref, quench_ref, gx * nrow + gy, w_ref)
     for copy in local:
@@ -220,28 +288,32 @@
             remote(west_send, west_recv, 7, east).wait_recv()
         left = west if step == 0 else west_recv
 
-        def block(i, carry):
-            base = pl.multiple_of(i * 256, 256)
-            rows = left[pl.ds(base, 256), :]
+        def spread_rows(k):
+            rows = left[k * 256 : (k + 1) * 256, :]
             for pair in range(8):
                 out = nt(rows, pt[pair * 256 : (pair + 1) * 256, :]).astype(BF)
-                fs[2 * pair] = out[:, 0:L]
-                fs[2 * pair + 1] = out[:, L : 2 * L]
+                fs[k, 2 * pair] = out[:, 0:L]
+                fs[k, 2 * pair + 1] = out[:, L : 2 * L]
+
+        def absorb(k):
             for pair in range(8):
                 cols = [
-                    jnp.concatenate([fs[d, u * B : (u + 1) * B, :] for d in range(B)], axis=0)
+                    jnp.concatenate([fs[k, d, u * B : (u + 1) * B, :] for d in range(B)], axis=0)
                     for u in (2 * pair, 2 * pair + 1)
                 ]
                 out = nn(w_ref[...], jnp.concatenate(cols, axis=1)).astype(BF)
-                for half in range(2):
-                    at = pl.ds(pl.multiple_of(base + (2 * pair + half) * B, B), B)
+                for side in range(2):
+                    at = k * 256 + (2 * pair + side) * B
                     for r in range(B):
-                        t_ref[r // 2, at, (r % 2) * L : (r % 2 + 1) * L] = out[
-                            r * B : (r + 1) * B, half * L : (half + 1) * L
+                        t_ref[r // 2, at : at + B, (r % 2) * L : (r % 2 + 1) * L] = out[
+                            r * B : (r + 1) * B, side * L : (side + 1) * L
                         ]
-            return carry
-
-        lax.fori_loop(0, 6, block, 0)
+
+        spread_rows(0)
+        for k in range(6):
+            if k < 5:
+                spread_rows(k + 1)
+            absorb(k)
 
         square = jnp.zeros((CHI, CHI), F32)
         blocks = []
@@ -268,8 +340,34 @@
         if step == STEPS - 1:
             for copy in corner_sends + [edge_send]:
                 copy.wait_recv()
-            for copy in corner_sends + [edge_send] + first_sends:
+            for copy in corner_sends + [edge_send] + first_sends[2:]:
                 copy.wait_send()
+            if spread:
+                @pl.when(first)
+                def _():
+                    for copy in chunk_sends(e_up_in, 0):
+                        copy.wait_send()
+
+                @pl.when(last)
+                def _():
+                    for copy in chunk_sends(e_low_in, 1):
+                        copy.wait_send()
+
+                @pl.when(jnp.logical_not(first))
+                def _():
+                    first_sends[0].wait_send()
+
+                @pl.when(jnp.logical_not(last))
+                def _():
+                    first_sends[1].wait_send()
+
+                @pl.when(helper)
+                def _():
+                    for copy in forwards:
+                        copy.wait_send()
+            else:
+                first_sends[0].wait_send()
+                first_sends[1].wait_send()
             remote(c_send, c_recv, 4, east).wait_send()
             remote(west_send, west_recv, 7, east).wait_send()
 
@@ -293,9 +391,11 @@
             natural, natural, natural, natural, natural, pltpu.VMEM((4, CHI, CHI), BF),
             tall, tall, tall, tall, four, four, four, pltpu.VMEM((256, 256), BF), inner, inner, inner,
             tall, tall, tall, tall, tall, tall, pltpu.VMEM((CHI * B, L), F32),
-            pltpu.VMEM((CHI, CHI * B), BF), tall, pltpu.VMEM((B, 256, L), BF),
+            pltpu.VMEM((CHI, CHI * B), BF), tall, pltpu.VMEM((6, B, 256, L), BF),
             pltpu.VMEM((8, CHI * B, 2 * L), BF), natural, pltpu.VMEM((2, CHI, CHI), BF),
+            pltpu.VMEM((2, CHI, L), BF),
             pltpu.SemaphoreType.DMA((5,)), pltpu.SemaphoreType.DMA((9,)), pltpu.SemaphoreType.DMA((9,)),
+            pltpu.SemaphoreType.DMA((CHUNKS,)), pltpu.SemaphoreType.DMA((2,)),
         ],
         compiler_params=pltpu.CompilerParams(
             collective_id=0, has_side_effects=True, vmem_limit_bytes=63 * 1024 * 1024

time: 88 us -> 69 us (0.78)
  Pallas kernels: 83.5 us -> 64.5 us
    pallas_call x1, Pallas kernels: 83.5 us -> 64.5 us  [per_device(): pl.pallas_call(kernel, out_shape=(corner, edge, corner), in_specs=[hbm] *...]
where the time goes in v2:
time: 69 us; the launch traced here: 68.8 us
  Pallas kernels  64.5 us (93%)
  local copies, waits for them, and re-layouts  3.66 us (5%)
    pallas_call x1, Pallas kernels, per_device(): pl.pallas_call(kernel, out_shape=(corner, edge, corner), in_specs=[hbm] *...  64.5 us
    unnamed x5, local copies, waits for them, and re-layouts  3.66 us

profile of v2, /device:TPU:1, one launch (start us, length us, event | category | flops | bytes accessed | tf_op | source)
XLA Modules:
  0.0 68.8 jit_solution(16057975585401827799)
XLA Ops:
  0.6 64.5 %left_move.1 = (bf16[1,1,96,96]{3,2,1,0:T(8,128)(2,1)}, bf16[1,1,96,1536]{3,2,1,0:T(8,128)(2,1)}, bf16[1,1,96,96]{3,2,1,0:T(8,128)(2,1)}) custom-call(bf16[1,1,96,96]{3,2,1,0:T(8,128)(2,1)} %c_up_in.1, bf16[1,1,96,1536]{3,2,1,0:T(8,128)(2,1)} %e_up_in.1, bf16[1,1,96,1536]{3,2,1,0:T(8,128)(2,1)} %e_left_in.1, bf16[1,1,96,96]{3,2,1,0:T(8,128)(2,1)} %c_low_in.1, ...), custom_call_target="tpu_custom_call" | custom-call | tf_op jit(solution)/shard_map/left_move/pallas_call | solution.py:385
  65.1 1.3 %copy.14 = bf16[1,1,96,96]{3,2,1,0:T(8,128)(2,1)} copy(bf16[1,1,96,96]{3,2,1,0:T(8,128)(2,1)} %get-tuple-element.6) | data formatting | bytes 36864
  66.4 0.0 copy-start
  66.4 1.7 %copy.15 = bf16[1,1,96,1536]{3,2,1,0:T(8,128)(2,1)} copy(bf16[1,1,96,1536]{3,2,1,0:T(8,128)(2,1)} %get-tuple-element.7) | data formatting | bytes 589824
  68.1 0.0 copy-done
  68.1 0.6 copy.16
Async XLA Ops:
  66.4 1.7 %copy-start = (bf16[1,1,96,96]{3,2,1,0:T(8,128)(2,1)S(1)}, bf16[1,1,96,96]{3,2,1,0:T(8,128)(2,1)}, u32[]{:S(2)}) copy-start(bf16[1,1,96,96]{3,2,1,0:T(8,128)(2,1)} %get-tuple-element.8) | copy-start | bytes 55300

commit v3 on v2

v3 whole, which is shorter than its diff:
```python
import jax
import jax.numpy as jnp
from jax import lax
from jax.experimental import pallas as pl
from jax.experimental.pallas import tpu as pltpu
from jax.sharding import PartitionSpec as P

NS_ITERS = 6
STEPS = 2
MESH = pl.DeviceIdType.MESH
CHI = 96
B = 16
HALF = 16
CHUNKS = 12
L = 128
F32 = jnp.float32
BF = jnp.bfloat16


def nt(a, b):
    return lax.dot_general(a, b, (((1,), (1,)), ((), ())), preferred_element_type=F32)


def nn(a, b):
    return jnp.dot(a, b, preferred_element_type=F32)


def split(x):
    hi = x.astype(BF)
    return hi, (x - hi.astype(F32)).astype(BF)


def product(a, b):
    a_hi, a_lo = split(a)
    b_hi, b_lo = split(b)
    return nn(
        jnp.concatenate([a_hi, a_lo], axis=1), jnp.concatenate([b_hi, b_hi], axis=0)
    ) + nn(a_hi, b_lo)


def eye():
    row = lax.broadcasted_iota(jnp.int32, (L, L), 0)
    col = lax.broadcasted_iota(jnp.int32, (L, L), 1)
    return jnp.where((row == col) & (row < CHI), 1.0, 0.0).astype(F32)


def polar_right(gram):
    one = eye()
    scale = 1.0 / (jnp.sum(gram * one) + 1e-06)
    s = gram * scale
    p = 1.5 * one - 0.5 * s
    m = p
    for _ in range(NS_ITERS - 1):
        s = product(product(s, p), p)
        p = 1.5 * one - 0.5 * s
        m = product(m, p)
    return m * jnp.sqrt(scale)


def unit_corner(x):
    return (x * lax.rsqrt(jnp.sum(x * x) * (1.0 / (CHI * CHI)) + 1e-06)).astype(BF)


def transposed_edge(edge_ref, out_ref):
    for chunk in range(4):
        lanes = edge_ref[:, chunk * 384 : (chunk + 1) * 384]
        lanes = jnp.concatenate([lanes, jnp.zeros((L - CHI, 384), BF)], axis=0)
        turned = lanes.T
        for i in range(4):
            d = chunk * 4 + i
            out_ref[d * L : d * L + CHI, :] = turned[i * CHI : (i + 1) * CHI, :]
            out_ref[d * L + CHI : (d + 1) * L, :] = jnp.zeros((L - CHI, L), BF)


def double_layer(ket_ref, gate_ref, quench_ref, own_index, mirror, out_ref):
    n = lax.broadcasted_iota(jnp.int32, (256, 256), 0)
    m = lax.broadcasted_iota(jnp.int32, (256, 256), 1)
    f4 = lambda x, k: (x >> (6 - 2 * k)) & 3
    outer = jnp.where(mirror, f4(m, 3), f4(m, 1))
    inner = jnp.where(mirror, f4(n, 1), f4(n, 3))
    ket_mask = (f4(n, 2) == outer) & (f4(n, 0) == f4(m, 2))
    bra_mask = (f4(n, 3) == outer) & (f4(n, 1) == f4(m, 2))
    ket_spread = ((f4(n, 0) == f4(m, 2)) & (inner == f4(m, 0))).astype(F32).astype(BF)
    bra_spread = ((f4(n, 0) == f4(m, 3)) & (inner == f4(m, 1))).astype(F32).astype(BF)
    chosen = quench_ref[0] == own_index
    for i in range(1, 4):
        chosen = chosen | (quench_ref[i] == own_index)
    kets = [ket_ref[0, 0, s : s + 1, :].astype(F32) for s in range(2)]
    total = jnp.zeros((256, 256), F32)
    for s in range(2):
        bra = jnp.zeros((1, 256), F32)
        for t in range(2):
            gram = gate_ref[0, s] * gate_ref[0, t] + gate_ref[1, s] * gate_ref[1, t]
            weight = jnp.where(chosen, gram, 1.0 if s == t else 0.0)
            bra = bra + weight * kets[t]
        bra = bra.astype(BF).astype(F32)
        ket_part = nn(jnp.where(ket_mask, kets[s], 0.0).astype(BF), ket_spread)
        bra_part = nn(jnp.where(bra_mask, bra, 0.0).astype(BF), bra_spread)
        total = total + ket_part * bra_part
    out_ref[...] = total.astype(BF)


def kernel(
    c_up_in, e_up_in, e_left_in, c_low_in, e_low_in, ket_ref, gate_ref, quench_ref,
    c_up_out, e_out, c_low_out,
    own, near, west_nat, c_in, et_own, et_near, cpad, c_send, c_recv, w_ref,
    west, west_recv, west_send, glu, inter, pup, pt, fs, t_ref, fin, e_fin, c_fin,
    hop, lsem, ssem, rsem, psem, hsem,
):
    gx, gy = lax.axis_index("gx"), lax.axis_index("gy")
    ncol, nrow = lax.axis_size("gx"), lax.axis_size("gy")
    north = (gx, lax.rem(gy + nrow - 1, nrow))
    south = (gx, lax.rem(gy + 1, nrow))
    east = (lax.rem(gx + 1, ncol), gy)
    before = (lax.rem(gx + ncol - 1, ncol), gy)
    spread = nrow == 2 * HALF
    period = HALF if spread else nrow
    half, place = gy // period, lax.rem(gy, period)
    first, last = place == 0, place == period - 1
    helper = (place >= 2) & (place < 2 + CHUNKS)
    mirror = last
    flip = jnp.where(mirror, 1, 0)
    barrier = pltpu.get_barrier_semaphore()

    def greet(peer):
        pl.semaphore_signal(barrier, inc=1, device_id=peer, device_id_type=MESH)

    for peer in (north, south, east, before):
        greet(peer)
    greeted = 4
    if spread:
        @pl.when(first | last)
        def _():
            for c in range(CHUNKS):
                greet((gx, 2 + c))
                greet((gx, HALF + 2 + c))

        @pl.when(helper)
        def _():
            for row in (0, HALF - 1, HALF, 2 * HALF - 1):
                greet((gx, row))

        greeted = 4 + jnp.where(helper, 4, 0) + jnp.where(first | last, 2 * CHUNKS, 0)

    local = [
        pltpu.make_async_copy(src.at[0, 0], dst, lsem.at[i])
        for i, (src, dst) in enumerate((
            (e_low_in, own.at[flip]), (e_up_in, own.at[1 - flip]), (e_left_in, west_nat),
            (c_low_in, c_in.at[2 * flip]), (c_up_in, c_in.at[2 - 2 * flip]),
        ))
    ]
    for copy in local:
        copy.start()
    pl.semaphore_wait(barrier, greeted)

    def remote(src, dst, i, peer, j=None):
        return pltpu.make_async_remote_copy(
            src_ref=src, dst_ref=dst, send_sem=ssem.at[i], recv_sem=rsem.at[i if j is None else j],
            device_id=peer, device_id_type=MESH,
        )

    to_north = jnp.where(first, 1, 0)
    to_south = jnp.where(place == period - 2, 0, 1)
    first_sends = [
        remote(e_up_in.at[0, 0], near.at[to_north], 0, north, to_north),
        remote(e_low_in.at[0, 0], near.at[to_south], 1, south, to_south),
        remote(c_up_in.at[0, 0], c_in.at[1 + 2 * to_north], 2, north, 2 + to_north),
        remote(c_low_in.at[0, 0], c_in.at[1 + 2 * to_south], 3, south, 2 + to_south),
    ]

    def relay(src, dst, send, recv, peer):
        return pltpu.make_async_remote_copy(
            src_ref=src, dst_ref=dst, send_sem=psem.at[send], recv_sem=recv,
            device_id=peer, device_id_type=MESH,
        )

    def chunk_sends(edge_in, slot):
        return [
            relay(edge_in.at[0, 0, :, pl.ds(c * L, L)], hop.at[slot], c, hsem.at[slot], (gx, half * HALF + 2 + c))
            for c in range(CHUNKS)
        ]

    lanes = pl.ds(pl.multiple_of((place - 2) * L, L), L)

    def forwards():
        return [
            relay(hop.at[0], near.at[1, :, lanes], 0, rsem.at[1], (gx, (1 - half) * HALF + HALF - 1)),
            relay(hop.at[1], near.at[1, :, lanes], 1, rsem.at[1], (gx, (1 - half) * HALF)),
        ]

    def forward():
        for slot, copy in enumerate(forwards()):
            relay(hop.at[slot], hop.at[slot], slot, hsem.at[slot], north).wait_recv()
            copy.start()

    if spread:
        @pl.when(first)
        def _():
            for copy in chunk_sends(e_up_in, 0):
                copy.start()

        @pl.when(last)
        def _():
            for copy in chunk_sends(e_low_in, 1):
                copy.start()

        @pl.when(jnp.logical_not(first))
        def _():
            first_sends[0].start()

        @pl.when(jnp.logical_not(last))
        def _():
            first_sends[1].start()
    else:
        first_sends[0].start()
        first_sends[1].start()
    first_sends[2].start()
    first_sends[3].start()
    if spread:
        @pl.when(helper & (half == 1))
        def _():
            forward()

    double_layer(ket_ref, gate_ref, quench_ref, gx * nrow + gy, mirror, w_ref)
    for copy in local:
        copy.wait()
    for cut in (0, 1):
        transposed_edge(own.at[cut], et_own.at[cut])

    def interleave(turned):
        for l in range(B):
            value = jnp.concatenate(
                [west_nat[:, l * CHI : (l + 1) * CHI].astype(F32), jnp.zeros((CHI, L - CHI), F32)], axis=1
            )
            if turned:
                value = jnp.concatenate([value, jnp.zeros((L - CHI, L), F32)], axis=0).T[0:CHI, :]
            inter[pl.ds(l, CHI, stride=B), :] = value

    @pl.when(mirror)
    def _():
        interleave(True)

    @pl.when(jnp.logical_not(mirror))
    def _():
        interleave(False)

    west[...] = inter[...].astype(BF)

    def arrive(cut):
        remote(near.at[cut], near.at[cut], cut, north).wait_recv()
        remote(c_in.at[0], c_in.at[0], 2 + cut, north).wait_recv()
        for i in (2 * cut, 2 * cut + 1):
            cpad[i] = jnp.zeros((L, L), BF)
            cpad[i, 0:CHI, :] = jnp.concatenate([c_in[i], jnp.zeros((CHI, L - CHI), BF)], axis=1)
        transposed_edge(near.at[cut], et_near.at[cut])

    def corner_send(cut):
        pair = pl.ds(2 * cut, 2)
        return remote(c_send.at[pair], c_recv.at[pair], 4 + cut, east)

    last_corners = [
        remote(c_fin.at[flip], c_low_out.at[0, 0], 7, east),
        remote(c_fin.at[1 - flip], c_up_out.at[0, 0], 8, east),
    ]

    def chain(step, cut):
        if step == 0:
            arrive(cut)
        else:
            corner_send(cut).wait_recv()
        corners = cpad if step == 0 else c_recv
        for piece in range(8):
            rows = slice(piece * 256, (piece + 1) * 256)
            mine = nt(et_own[cut, rows, :], corners[2 * cut])
            other = nt(et_near[cut, rows, :], corners[2 * cut + 1])
            for i, value in enumerate(((mine + other), mine, other)):
                value = value.astype(BF)
                for side in range(2):
                    at = piece * 256 + side * L
                    glu[i * L : (i + 1) * L, at : at + L] = value[side * L : (side + 1) * L, :]
        sums = nt(glu[0:L, :], glu[...])
        if cut == 1:
            for d in range(B):
                rows = slice(d * L, (d + 1) * L)
                value = nt(corners[2], et_own[1, rows, :]) + nt(corners[3], et_near[1, rows, :])
                inter[pl.ds(d, CHI, stride=B), :] = value[0:CHI, :]
        m = polar_right(sums[:, 0:L])
        new_own = unit_corner(product(m, sums[:, L : 2 * L]))
        if step < STEPS - 1:
            c_send[2 * cut] = new_own
            c_send[2 * cut + 1] = unit_corner(product(m, sums[:, 2 * L : 3 * L]))
            corner_send(cut).start()
        else:
            c_fin[cut] = new_own[0:CHI, 0:CHI]
        m_rows = jnp.concatenate(list(split(m)), axis=0)
        if cut == 0:
            for piece in range(8):
                both = nn(m_rows, glu[0:L, piece * 256 : (piece + 1) * 256])
                both = (both[0:L] + both[L : 2 * L]).astype(BF)
                for side in range(2):
                    at = piece * 256 + side * L
                    pt[at : at + L, :] = both[:, side * L : (side + 1) * L]
        else:
            for piece in range(6):
                rows = slice(piece * 256, (piece + 1) * 256)
                both = nt(m_rows, inter[rows, :].astype(BF))
                pup[:, rows] = (both[0:CHI] + both[L : L + CHI]).astype(BF)

    def contract(left):
        def spread_rows(k):
            rows = left[k * 256 : (k + 1) * 256, :]
            for pair in range(8):
                out = nt(rows, pt[pair * 256 : (pair + 1) * 256, :]).astype(BF)
                fs[k, 2 * pair] = out[:, 0:L]
                fs[k, 2 * pair + 1] = out[:, L : 2 * L]

        def absorb(k):
            for pair in range(8):
                cols = [
                    jnp.concatenate([fs[k, d, u * B : (u + 1) * B, :] for d in range(B)], axis=0)
                    for u in (2 * pair, 2 * pair + 1)
                ]
                out = nn(w_ref[...], jnp.concatenate(cols, axis=1)).astype(BF)
                for side in range(2):
                    at = k * 256 + (2 * pair + side) * B
                    for r in range(B):
                        t_ref[r // 2, at : at + B, (r % 2) * L : (r % 2 + 1) * L] = out[
                            r * B : (r + 1) * B, side * L : (side + 1) * L
                        ]

        spread_rows(0)
        for k in range(6):
            if k < 5:
                spread_rows(k + 1)
            absorb(k)

    def close(store):
        square = jnp.zeros((CHI, CHI), F32)
        for pair in range(8):
            out = nn(pup[...], t_ref[pair])
            for side in range(2):
                value = out[:, side * L : side * L + CHI]
                square = square + value * value
                store(2 * pair + side, jnp.concatenate([value, jnp.zeros((CHI, L - CHI), F32)], axis=1))
        return lax.rsqrt(jnp.sum(square) * (1.0 / (CHI * CHI * B)) + 1e-06)

    chain(0, 0)
    contract(west)
    chain(1, 0)
    if spread:
        @pl.when(helper & (half == 0))
        def _():
            forward()

    chain(0, 1)

    def store_west(r, value):
        inter[pl.ds(r, CHI, stride=B), :] = value

    scale = close(store_west)
    west_send[...] = (inter[...] * scale).astype(BF)
    west_shift = remote(west_send, west_recv, 6, east)
    west_shift.start()
    chain(1, 1)
    for copy in last_corners:
        copy.start()
    west_shift.wait_recv()
    contract(west_recv)

    def store_last(r, value):
        fin[r, 0:CHI, :] = value

    scale = close(store_last)

    @pl.when(mirror)
    def _():
        e_fin[...] = jnp.concatenate([(fin[r].T[0:CHI, 0:CHI] * scale).astype(BF) for r in range(B)], axis=1)

    @pl.when(jnp.logical_not(mirror))
    def _():
        e_fin[...] = jnp.concatenate([(fin[r, 0:CHI, 0:CHI] * scale).astype(BF) for r in range(B)], axis=1)

    edge_shift = remote(e_fin, e_out.at[0, 0], 9, east)
    edge_shift.start()
    for copy in last_corners + [edge_shift]:
        copy.wait_recv()
    for copy in last_corners + [edge_shift, west_shift, corner_send(0), corner_send(1)] + first_sends[2:]:
        copy.wait_send()
    if spread:
        @pl.when(first)
        def _():
            for copy in chunk_sends(e_up_in, 0):
                copy.wait_send()

        @pl.when(last)
        def _():
            for copy in chunk_sends(e_low_in, 1):
                copy.wait_send()

        @pl.when(jnp.logical_not(first))
        def _():
            first_sends[0].wait_send()

        @pl.when(jnp.logical_not(last))
        def _():
            first_sends[1].wait_send()

        @pl.when(helper)
        def _():
            for copy in forwards():
                copy.wait_send()
    else:
        first_sends[0].wait_send()
        first_sends[1].wait_send()


def per_device(c_upper, edge_upper, edge_left, c_lower, edge_lower, site_ket, time_gate, quench_sites):
    hbm = pl.BlockSpec(memory_space=pl.ANY)
    vmem = pl.BlockSpec(memory_space=pltpu.VMEM)
    smem = pl.BlockSpec(memory_space=pltpu.SMEM)
    corner = jax.ShapeDtypeStruct((1, 1, CHI, CHI), BF)
    edge = jax.ShapeDtypeStruct((1, 1, CHI, B * CHI), BF)
    inner = pltpu.VMEM((CHI * B, L), BF)
    four = pltpu.VMEM((4, L, L), BF)
    two_edges = pltpu.VMEM((2, CHI, B * CHI), BF)
    two_tall = pltpu.VMEM((2, B * L, L), BF)
    dma = pltpu.SemaphoreType.DMA
    return pl.pallas_call(
        kernel,
        out_shape=(corner, edge, corner),
        in_specs=[hbm] * 5 + [vmem, smem, smem],
        out_specs=(hbm,) * 3,
        scratch_shapes=[
            two_edges, two_edges, pltpu.VMEM((CHI, B * CHI), BF), pltpu.VMEM((4, CHI, CHI), BF),
            two_tall, two_tall, four, four, four, pltpu.VMEM((256, 256), BF),
            inner, inner, inner, pltpu.VMEM((3 * L, B * L), BF), pltpu.VMEM((CHI * B, L), F32),
            pltpu.VMEM((CHI, CHI * B), BF), pltpu.VMEM((B * L, L), BF), pltpu.VMEM((6, B, 256, L), BF),
            pltpu.VMEM((8, CHI * B, 2 * L), BF), pltpu.VMEM((B, L, L), F32),
            pltpu.VMEM((CHI, B * CHI), BF), pltpu.VMEM((2, CHI, CHI), BF),
            pltpu.VMEM((2, CHI, L), BF),
            dma((5,)), dma((10,)), dma((10,)), dma((CHUNKS,)), dma((2,)),
        ],
        compiler_params=pltpu.CompilerParams(
            collective_id=0, has_side_effects=True, vmem_limit_bytes=63 * 1024 * 1024
        ),
        name="left_move",
    )(c_upper, edge_upper, edge_left, c_lower, edge_lower, site_ket, time_gate, quench_sites)


def solution(mesh):
    site = P("gx", "gy", None, None)
    return jax.shard_map(
        per_device,
        mesh=mesh,
        in_specs=(site,) * 6 + (P(), P()),
        out_specs=(site,) * 3,
        check_vma=False,
    )
```

time: 69 us -> 67.9 us (0.984)
  the two profiles are of different devices: /device:TPU:1 before, /device:TPU:384 now
where the time goes in v3:
time: 67.9 us; the launch traced here: 67.7 us
  Pallas kernels  63.4 us (93%)
  local copies, waits for them, and re-layouts  3.66 us (5%)
    pallas_call x1, Pallas kernels, per_device(): pl.pallas_call(kernel, out_shape=(corner, edge, corner), in_specs=[hbm] *...  63.4 us
    unnamed x5, local copies, waits for them, and re-layouts  3.66 us

profile of v3, /device:TPU:384, one launch (start us, length us, event | category | flops | bytes accessed | tf_op | source)
XLA Modules:
  0.0 67.7 jit_solution(8154406039048541616)
XLA Ops:
  0.6 63.4 %left_move.1 = (bf16[1,1,96,96]{3,2,1,0:T(8,128)(2,1)}, bf16[1,1,96,1536]{3,2,1,0:T(8,128)(2,1)}, bf16[1,1,96,96]{3,2,1,0:T(8,128)(2,1)}) custom-call(bf16[1,1,96,96]{3,2,1,0:T(8,128)(2,1)} %c_up_in.1, bf16[1,1,96,1536]{3,2,1,0:T(8,128)(2,1)} %e_up_in.1, bf16[1,1,96,1536]{3,2,1,0:T(8,128)(2,1)} %e_left_in.1, bf16[1,1,96,96]{3,2,1,0:T(8,128)(2,1)} %c_low_in.1, ...), custom_call_target="tpu_custom_call" | custom-call | tf_op jit(solution)/shard_map/left_move/pallas_call | solution.py:428
  64.1 1.3 %copy.14 = bf16[1,1,96,96]{3,2,1,0:T(8,128)(2,1)} copy(bf16[1,1,96,96]{3,2,1,0:T(8,128)(2,1)} %get-tuple-element.6) | data formatting | bytes 36864
  65.4 0.0 copy-start
  65.4 1.7 %copy.15 = bf16[1,1,96,1536]{3,2,1,0:T(8,128)(2,1)} copy(bf16[1,1,96,1536]{3,2,1,0:T(8,128)(2,1)} %get-tuple-element.7) | data formatting | bytes 589824
  67.1 0.0 copy-done
  67.1 0.6 copy.16
Async XLA Ops:
  65.4 1.7 %copy-start = (bf16[1,1,96,96]{3,2,1,0:T(8,128)(2,1)S(1)}, bf16[1,1,96,96]{3,2,1,0:T(8,128)(2,1)}, u32[]{:S(2)}) copy-start(bf16[1,1,96,96]{3,2,1,0:T(8,128)(2,1)} %get-tuple-element.8) | copy-start | bytes 55300

commit v4 on v3

--- a/solution.py
+++ b/solution.py
@@ -105,7 +105,7 @@
     c_up_out, e_out, c_low_out,
     own, near, west_nat, c_in, et_own, et_near, cpad, c_send, c_recv, w_ref,
     west, west_recv, west_send, glu, inter, pup, pt, fs, t_ref, fin, e_fin, c_fin,
-    hop, lsem, ssem, rsem, psem, hsem,
+    hop, lsem, ssem, rsem, psem, hsem, ready,
 ):
     gx, gy = lax.axis_index("gx"), lax.axis_index("gy")
     ncol, nrow = lax.axis_size("gx"), lax.axis_size("gy")
@@ -125,22 +125,44 @@
     def greet(peer):
         pl.semaphore_signal(barrier, inc=1, device_id=peer, device_id_type=MESH)
 
-    for peer in (north, south, east, before):
-        greet(peer)
-    greeted = 4
+    edge_row = first | last
+    far = jnp.where(first, (1 - half) * HALF + HALF - 1, (1 - half) * HALF)
+    greet(before)
     if spread:
-        @pl.when(first | last)
+        @pl.when(jnp.logical_not(first & (half == 1)))
+        def _():
+            greet(north)
+
+        @pl.when(jnp.logical_not(last & (half == 1)))
+        def _():
+            greet(south)
+
+        @pl.when(edge_row & (half == 0))
         def _():
             for c in range(CHUNKS):
-                greet((gx, 2 + c))
                 greet((gx, HALF + 2 + c))
 
         @pl.when(helper)
         def _():
-            for row in (0, HALF - 1, HALF, 2 * HALF - 1):
-                greet((gx, row))
-
-        greeted = 4 + jnp.where(helper, 4, 0) + jnp.where(first | last, 2 * CHUNKS, 0)
+            greet((gx, half * HALF))
+            greet((gx, half * HALF + HALF - 1))
+
+        @pl.when(helper & (half == 0))
+        def _():
+            greet((gx, HALF))
+            greet((gx, 2 * HALF - 1))
+
+        greeted = (
+            3
+            + jnp.where(helper & (half == 1), 2, 0)
+            + jnp.where(edge_row, CHUNKS, 0)
+            + jnp.where(edge_row & (half == 1), CHUNKS, 0)
+            - jnp.where(edge_row & (half == 0), 1, 0)
+        )
+    else:
+        greet(north)
+        greet(south)
+        greeted = 3
 
     local = [
         pltpu.make_async_copy(src.at[0, 0], dst, lsem.at[i])
@@ -152,6 +174,12 @@
     for copy in local:
         copy.start()
     pl.semaphore_wait(barrier, greeted)
+    if spread:
+        @pl.when(edge_row & (half == 1))
+        def _():
+            for row in [far] + [2 + c for c in range(CHUNKS)]:
+                pl.semaphore_signal(ready, inc=1, device_id=(gx, row), device_id_type=MESH)
+
 
     def remote(src, dst, i, peer, j=None):
         return pltpu.make_async_remote_copy(
@@ -189,6 +217,10 @@
         ]
 
     def forward():
+        @pl.when(half == 0)
+        def _():
+            pl.semaphore_wait(ready, 2)
+
         for slot, copy in enumerate(forwards()):
             relay(hop.at[slot], hop.at[slot], slot, hsem.at[slot], north).wait_recv()
             copy.start()
@@ -214,9 +246,17 @@
     else:
         first_sends[0].start()
         first_sends[1].start()
-    first_sends[2].start()
-    first_sends[3].start()
+        first_sends[2].start()
+        first_sends[3].start()
     if spread:
+        @pl.when(jnp.logical_not(first & (half == 0)))
+        def _():
+            first_sends[2].start()
+
+        @pl.when(jnp.logical_not(last & (half == 0)))
+        def _():
+            first_sends[3].start()
+
         @pl.when(helper & (half == 1))
         def _():
             forward()
@@ -348,6 +388,16 @@
     contract(west)
     chain(1, 0)
     if spread:
+        @pl.when(first & (half == 0))
+        def _():
+            pl.semaphore_wait(ready, 1)
+            first_sends[2].start()
+
+        @pl.when(last & (half == 0))
+        def _():
+            pl.semaphore_wait(ready, 1)
+            first_sends[3].start()
+
         @pl.when(helper & (half == 0))
         def _():
             forward()
@@ -412,6 +462,19 @@
     else:
         first_sends[0].wait_send()
         first_sends[1].wait_send()
+
+
+def settle(*refs):
+    sources, targets, stages, sem = refs[0:3], refs[3:6], refs[6:9], refs[9]
+    fetch = [pltpu.make_async_copy(sources[i], stages[i], sem.at[i]) for i in range(3)]
+    keep = [pltpu.make_async_copy(stages[i], targets[i], sem.at[3 + i]) for i in range(3)]
+    for copy in fetch:
+        copy.start()
+    for i in (0, 2, 1):
+        fetch[i].wait()
+        keep[i].start()
+    for copy in keep:
+        copy.wait()
 
 
 def per_device(c_upper, edge_upper, edge_left, c_lower, edge_lower, site_ket, time_gate, quench_sites):
@@ -425,7 +488,7 @@
     two_edges = pltpu.VMEM((2, CHI, B * CHI), BF)
     two_tall = pltpu.VMEM((2, B * L, L), BF)
     dma = pltpu.SemaphoreType.DMA
-    return pl.pallas_call(
+    moved = pl.pallas_call(
         kernel,
         out_shape=(corner, edge, corner),
         in_specs=[hbm] * 5 + [vmem, smem, smem],
@@ -439,12 +502,25 @@
             pltpu.VMEM((CHI, B * CHI), BF), pltpu.VMEM((2, CHI, CHI), BF),
             pltpu.VMEM((2, CHI, L), BF),
             dma((5,)), dma((10,)), dma((10,)), dma((CHUNKS,)), dma((2,)),
+            pltpu.SemaphoreType.REGULAR,
         ],
         compiler_params=pltpu.CompilerParams(
             collective_id=0, has_side_effects=True, vmem_limit_bytes=63 * 1024 * 1024
         ),
         name="left_move",
     )(c_upper, edge_upper, edge_left, c_lower, edge_lower, site_ket, time_gate, quench_sites)
+    return pl.pallas_call(
+        settle,
+        out_shape=(corner, edge, corner),
+        in_specs=[hbm] * 3,
+        out_specs=(hbm,) * 3,
+        scratch_shapes=[
+            pltpu.VMEM((1, 1, CHI, CHI), BF), pltpu.VMEM((1, 1, CHI, B * CHI), BF), pltpu.VMEM((1, 1, CHI, CHI), BF),
+            pltpu.SemaphoreType.DMA((6,)),
+        ],
+        compiler_params=pltpu.CompilerParams(vmem_limit_bytes=63 * 1024 * 1024),
+        name="settle",
+    )(*moved)
 
 
 def solution(mesh):

time: 67.9 us -> 63.3 us (0.932)
  the two profiles are of different devices: /device:TPU:384 before, /device:TPU:1 now
where the time goes in v4:
time: 63.3 us; the launch traced here: 63.1 us
  Pallas kernels  62.3 us (98%)
  between operations  0.8 us (1%)
    pallas_call x1, Pallas kernels, per_device(): pl.pallas_call(kernel, out_shape=(corner, edge, corner), in_specs=[hbm] *...  60.6 us
    pallas_call x1, Pallas kernels, per_device(): pl.pallas_call(settle, out_shape=(corner, edge, corner), in_specs=[hbm] *...  1.75 us

profile of v4, /device:TPU:1, one launch (start us, length us, event | category | flops | bytes accessed | tf_op | source)
XLA Modules:
  0.0 63.1 jit_solution(11152736767468359796)
XLA Ops:
  0.6 60.6 %left_move.1 = (bf16[1,1,96,96]{3,2,1,0:T(8,128)(2,1)}, bf16[1,1,96,1536]{3,2,1,0:T(8,128)(2,1)}, bf16[1,1,96,96]{3,2,1,0:T(8,128)(2,1)}) custom-call(bf16[1,1,96,96]{3,2,1,0:T(8,128)(2,1)} %c_up_in.1, bf16[1,1,96,1536]{3,2,1,0:T(8,128)(2,1)} %e_up_in.1, bf16[1,1,96,1536]{3,2,1,0:T(8,128)(2,1)} %e_left_in.1, bf16[1,1,96,96]{3,2,1,0:T(8,128)(2,1)} %c_low_in.1, ...), custom_call_target="tpu_custom_call" | custom-call | tf_op jit(solution)/shard_map/left_move/pallas_call | solution.py:491
  61.2 1.7 %settle.1 = (bf16[1,1,96,96]{3,2,1,0:T(8,128)(2,1)}, bf16[1,1,96,1536]{3,2,1,0:T(8,128)(2,1)}, bf16[1,1,96,96]{3,2,1,0:T(8,128)(2,1)}) custom-call(bf16[1,1,96,96]{3,2,1,0:T(8,128)(2,1)} %get-tuple-element.6.refs_0_, bf16[1,1,96,1536]{3,2,1,0:T(8,128)(2,1)} %get-tuple-element.7.refs_1_, bf16[1,1,96,96]{3,2,1,0:T(8,128)(2,1)} %get-tuple-element.8.refs_2_), custom_call_target="tpu_custom_call" | custom-call | tf_op jit(solution)/shard_map/settle/pallas_call | solution.py:512

commit v5 on v4

--- a/solution.py
+++ b/solution.py
@@ -105,7 +105,7 @@
     c_up_out, e_out, c_low_out,
     own, near, west_nat, c_in, et_own, et_near, cpad, c_send, c_recv, w_ref,
     west, west_recv, west_send, glu, inter, pup, pt, fs, t_ref, fin, e_fin, c_fin,
-    hop, lsem, ssem, rsem, psem, hsem, ready,
+    hop, lsem, ssem, rsem, psem, hsem, wsend, wrecv, ready,
 ):
     gx, gy = lax.axis_index("gx"), lax.axis_index("gy")
     ncol, nrow = lax.axis_size("gx"), lax.axis_size("gy")
@@ -226,15 +226,33 @@
             copy.start()
 
     if spread:
+        @pl.when(jnp.logical_not(first & (half == 0)))
+        def _():
+            first_sends[2].start()
+
+        @pl.when(jnp.logical_not(last & (half == 0)))
+        def _():
+            first_sends[3].start()
+
         @pl.when(first)
         def _():
-            for copy in chunk_sends(e_up_in, 0):
+            copies = chunk_sends(e_up_in, 0)
+            for copy in copies:
                 copy.start()
+            for copy in copies:
+                copy.wait_send()
 
         @pl.when(last)
         def _():
-            for copy in chunk_sends(e_low_in, 1):
+            copies = chunk_sends(e_low_in, 1)
+            for copy in copies:
                 copy.start()
+            for copy in copies:
+                copy.wait_send()
+
+        @pl.when(helper & (half == 1))
+        def _():
+            forward()
 
         @pl.when(jnp.logical_not(first))
         def _():
@@ -244,22 +262,8 @@
         def _():
             first_sends[1].start()
     else:
-        first_sends[0].start()
-        first_sends[1].start()
-        first_sends[2].start()
-        first_sends[3].start()
-    if spread:
-        @pl.when(jnp.logical_not(first & (half == 0)))
-        def _():
-            first_sends[2].start()
-
-        @pl.when(jnp.logical_not(last & (half == 0)))
-        def _():
-            first_sends[3].start()
-
-        @pl.when(helper & (half == 1))
-        def _():
-            forward()
+        for copy in first_sends:
+            copy.start()
 
     double_layer(ket_ref, gate_ref, quench_ref, gx * nrow + gy, mirror, w_ref)
     for copy in local:
@@ -346,8 +350,10 @@
                 both = nt(m_rows, inter[rows, :].astype(BF))
                 pup[:, rows] = (both[0:CHI] + both[L : L + CHI]).astype(BF)
 
-    def contract(left):
+    def contract(left, arrivals=None):
         def spread_rows(k):
+            if arrivals is not None and k % 2 == 0:
+                arrivals[k // 2].wait_recv()
             rows = left[k * 256 : (k + 1) * 256, :]
             for pair in range(8):
                 out = nt(rows, pt[pair * 256 : (pair + 1) * 256, :]).astype(BF)
@@ -408,14 +414,21 @@
         inter[pl.ds(r, CHI, stride=B), :] = value
 
     scale = close(store_west)
-    west_send[...] = (inter[...] * scale).astype(BF)
-    west_shift = remote(west_send, west_recv, 6, east)
-    west_shift.start()
+    west_shift = []
+    for k in range(3):
+        rows = pl.ds(k * 512, 512)
+        west_send[rows, :] = (inter[rows, :] * scale).astype(BF)
+        west_shift.append(
+            pltpu.make_async_remote_copy(
+                src_ref=west_send.at[rows], dst_ref=west_recv.at[rows], send_sem=wsend.at[k], recv_sem=wrecv.at[k],
+                device_id=east, device_id_type=MESH,
+            )
+        )
+        west_shift[k].start()
     chain(1, 1)
     for copy in last_corners:
         copy.start()
-    west_shift.wait_recv()
-    contract(west_recv)
+    contract(west_recv, west_shift)
 
     def store_last(r, value):
         fin[r, 0:CHI, :] = value
@@ -434,19 +447,9 @@
     edge_shift.start()
     for copy in last_corners + [edge_shift]:
         copy.wait_recv()
-    for copy in last_corners + [edge_shift, west_shift, corner_send(0), corner_send(1)] + first_sends[2:]:
+    for copy in last_corners + west_shift + [edge_shift, corner_send(0), corner_send(1)] + first_sends[2:]:
         copy.wait_send()
     if spread:
-        @pl.when(first)
-        def _():
-            for copy in chunk_sends(e_up_in, 0):
-                copy.wait_send()
-
-        @pl.when(last)
-        def _():
-            for copy in chunk_sends(e_low_in, 1):
-                copy.wait_send()
-
         @pl.when(jnp.logical_not(first))
         def _():
             first_sends[0].wait_send()
@@ -501,7 +504,7 @@
             pltpu.VMEM((8, CHI * B, 2 * L), BF), pltpu.VMEM((B, L, L), F32),
             pltpu.VMEM((CHI, B * CHI), BF), pltpu.VMEM((2, CHI, CHI), BF),
             pltpu.VMEM((2, CHI, L), BF),
-            dma((5,)), dma((10,)), dma((10,)), dma((CHUNKS,)), dma((2,)),
+            dma((5,)), dma((10,)), dma((10,)), dma((CHUNKS,)), dma((2,)), dma((3,)), dma((3,)),
             pltpu.SemaphoreType.REGULAR,
         ],
         compiler_params=pltpu.CompilerParams(

time: 63.3 us -> 61.5 us (0.972)
  the two profiles are of different devices: /device:TPU:1 before, /device:TPU:28 now
where the time goes in v5:
time: 61.5 us; the launch traced here: 61.4 us
  Pallas kernels  60.6 us (99%)
  between operations  0.8 us (1%)
    pallas_call x1, Pallas kernels, per_device(): pl.pallas_call(kernel, out_shape=(corner, edge, corner), in_specs=[hbm] *...  58.8 us
    pallas_call x1, Pallas kernels, per_device(): pl.pallas_call(settle, out_shape=(corner, edge, corner), in_specs=[hbm] *...  1.75 us

profile of v5, /device:TPU:28, one launch (start us, length us, event | category | flops | bytes accessed | tf_op | source)
XLA Modules:
  0.0 61.4 jit_solution(9127826395480265869)
XLA Ops:
  0.6 58.8 %left_move.1 = (bf16[1,1,96,96]{3,2,1,0:T(8,128)(2,1)}, bf16[1,1,96,1536]{3,2,1,0:T(8,128)(2,1)}, bf16[1,1,96,96]{3,2,1,0:T(8,128)(2,1)}) custom-call(bf16[1,1,96,96]{3,2,1,0:T(8,128)(2,1)} %c_up_in.1, bf16[1,1,96,1536]{3,2,1,0:T(8,128)(2,1)} %e_up_in.1, bf16[1,1,96,1536]{3,2,1,0:T(8,128)(2,1)} %e_left_in.1, bf16[1,1,96,96]{3,2,1,0:T(8,128)(2,1)} %c_low_in.1, ...), custom_call_target="tpu_custom_call" | custom-call | tf_op jit(solution)/shard_map/left_move/pallas_call | solution.py:494
  59.4 1.7 %settle.1 = (bf16[1,1,96,96]{3,2,1,0:T(8,128)(2,1)}, bf16[1,1,96,1536]{3,2,1,0:T(8,128)(2,1)}, bf16[1,1,96,96]{3,2,1,0:T(8,128)(2,1)}) custom-call(bf16[1,1,96,96]{3,2,1,0:T(8,128)(2,1)} %get-tuple-element.6.refs_0_, bf16[1,1,96,1536]{3,2,1,0:T(8,128)(2,1)} %get-tuple-element.7.refs_1_, bf16[1,1,96,96]{3,2,1,0:T(8,128)(2,1)} %get-tuple-element.8.refs_2_), custom_call_target="tpu_custom_call" | custom-call | tf_op jit(solution)/shard_map/settle/pallas_call | solution.py:515

commit v6 on v5

--- a/solution.py
+++ b/solution.py
@@ -234,6 +234,17 @@
         def _():
             first_sends[3].start()
 
+        def near_sends(side):
+            @pl.when(jnp.logical_not(first) & (half == side))
+            def _():
+                first_sends[0].start()
+
+            @pl.when(jnp.logical_not(last) & (half == side))
+            def _():
+                first_sends[1].start()
+
+        near_sends(0)
+
         @pl.when(first)
         def _():
             copies = chunk_sends(e_up_in, 0)
@@ -254,13 +265,7 @@
         def _():
             forward()
 
-        @pl.when(jnp.logical_not(first))
-        def _():
-            first_sends[0].start()
-
-        @pl.when(jnp.logical_not(last))
-        def _():
-            first_sends[1].start()
+        near_sends(1)
     else:
         for copy in first_sends:
             copy.start()
@@ -392,7 +397,11 @@
 
     chain(0, 0)
     contract(west)
-    chain(1, 0)
+
+    @pl.when(edge_row)
+    def _():
+        chain(1, 0)
+
     if spread:
         @pl.when(first & (half == 0))
         def _():
@@ -404,11 +413,11 @@
             pl.semaphore_wait(ready, 1)
             first_sends[3].start()
 
+    chain(0, 1)
+    if spread:
         @pl.when(helper & (half == 0))
         def _():
             forward()
-
-    chain(0, 1)
 
     def store_west(r, value):
         inter[pl.ds(r, CHI, stride=B), :] = value
@@ -425,6 +434,11 @@
             )
         )
         west_shift[k].start()
+
+    @pl.when(jnp.logical_not(edge_row))
+    def _():
+        chain(1, 0)
+
     chain(1, 1)
     for copy in last_corners:
         copy.start()

time: 61.5 us -> 62 us (level)
  the two profiles are of different devices: /device:TPU:28 before, /device:TPU:256 now
where the time goes in v6:
time: 62 us; the launch traced here: 61.8 us
  Pallas kernels  61 us (98%)
  between operations  0.8 us (1%)
    pallas_call x1, Pallas kernels, per_device(): pl.pallas_call(kernel, out_shape=(corner, edge, corner), in_specs=[hbm] *...  59.3 us
    pallas_call x1, Pallas kernels, per_device(): pl.pallas_call(settle, out_shape=(corner, edge, corner), in_specs=[hbm] *...  1.75 us

profile of v6, /device:TPU:256, one launch (start us, length us, event | category | flops | bytes accessed | tf_op | source)
XLA Modules:
  0.0 61.8 jit_solution(10883322575147115274)
XLA Ops:
  0.6 59.3 %left_move.1 = (bf16[1,1,96,96]{3,2,1,0:T(8,128)(2,1)}, bf16[1,1,96,1536]{3,2,1,0:T(8,128)(2,1)}, bf16[1,1,96,96]{3,2,1,0:T(8,128)(2,1)}) custom-call(bf16[1,1,96,96]{3,2,1,0:T(8,128)(2,1)} %c_up_in.1, bf16[1,1,96,1536]{3,2,1,0:T(8,128)(2,1)} %e_up_in.1, bf16[1,1,96,1536]{3,2,1,0:T(8,128)(2,1)} %e_left_in.1, bf16[1,1,96,96]{3,2,1,0:T(8,128)(2,1)} %c_low_in.1, ...), custom_call_target="tpu_custom_call" | custom-call | tf_op jit(solution)/shard_map/left_move/pallas_call | solution.py:508
  59.9 1.7 %settle.1 = (bf16[1,1,96,96]{3,2,1,0:T(8,128)(2,1)}, bf16[1,1,96,1536]{3,2,1,0:T(8,128)(2,1)}, bf16[1,1,96,96]{3,2,1,0:T(8,128)(2,1)}) custom-call(bf16[1,1,96,96]{3,2,1,0:T(8,128)(2,1)} %get-tuple-element.6.refs_0_, bf16[1,1,96,1536]{3,2,1,0:T(8,128)(2,1)} %get-tuple-element.7.refs_1_, bf16[1,1,96,96]{3,2,1,0:T(8,128)(2,1)} %get-tuple-element.8.refs_2_), custom_call_target="tpu_custom_call" | custom-call | tf_op jit(solution)/shard_map/settle/pallas_call | solution.py:529

commit v7 on v6

--- a/solution.py
+++ b/solution.py
@@ -413,11 +413,12 @@
             pl.semaphore_wait(ready, 1)
             first_sends[3].start()
 
-    chain(0, 1)
     if spread:
         @pl.when(helper & (half == 0))
         def _():
             forward()
+
+    chain(0, 1)
 
     def store_west(r, value):
         inter[pl.ds(r, CHI, stride=B), :] = value

time: 62 us -> 62 us (level)
  no operation moved by 1% of the time
where the time goes in v7:
time: 62 us; the launch traced here: 61.8 us
  Pallas kernels  61 us (98%)
  between operations  0.8 us (1%)
    pallas_call x1, Pallas kernels, per_device(): pl.pallas_call(kernel, out_shape=(corner, edge, corner), in_specs=[hbm] *...  59.3 us
    pallas_call x1, Pallas kernels, per_device(): pl.pallas_call(settle, out_shape=(corner, edge, corner), in_specs=[hbm] *...  1.75 us

profile of v7, /device:TPU:256, one launch (start us, length us, event | category | flops | bytes accessed | tf_op | source)
XLA Modules:
  0.0 61.8 jit_solution(3358591319584147856)
XLA Ops:
  0.6 59.3 %left_move.1 = (bf16[1,1,96,96]{3,2,1,0:T(8,128)(2,1)}, bf16[1,1,96,1536]{3,2,1,0:T(8,128)(2,1)}, bf16[1,1,96,96]{3,2,1,0:T(8,128)(2,1)}) custom-call(bf16[1,1,96,96]{3,2,1,0:T(8,128)(2,1)} %c_up_in.1, bf16[1,1,96,1536]{3,2,1,0:T(8,128)(2,1)} %e_up_in.1, bf16[1,1,96,1536]{3,2,1,0:T(8,128)(2,1)} %e_left_in.1, bf16[1,1,96,96]{3,2,1,0:T(8,128)(2,1)} %c_low_in.1, ...), custom_call_target="tpu_custom_call" | custom-call | tf_op jit(solution)/shard_map/left_move/pallas_call | solution.py:509
  59.9 1.7 %settle.1 = (bf16[1,1,96,96]{3,2,1,0:T(8,128)(2,1)}, bf16[1,1,96,1536]{3,2,1,0:T(8,128)(2,1)}, bf16[1,1,96,96]{3,2,1,0:T(8,128)(2,1)}) custom-call(bf16[1,1,96,96]{3,2,1,0:T(8,128)(2,1)} %get-tuple-element.6.refs_0_, bf16[1,1,96,1536]{3,2,1,0:T(8,128)(2,1)} %get-tuple-element.7.refs_1_, bf16[1,1,96,96]{3,2,1,0:T(8,128)(2,1)} %get-tuple-element.8.refs_2_), custom_call_target="tpu_custom_call" | custom-call | tf_op jit(solution)/shard_map/settle/pallas_call | solution.py:530
